TPU v7x, 32 devices: a whole 2x2x4 slice. The times are simulated.
32 devices in a mesh: row: 32 (over z, y, x, core), col: 1.
Axes of the slice: x: 2, y: 2, z: 4, core: 2. Of those that a mesh axis runs over, the one named last changes fastest.
Arguments:
- convolution_input: bfloat16 [256, 256, 128], P('row', 'col'), may hold values from -6 to 6
- pair: bfloat16 [256, 256, 128], P('row', 'col'), may hold values from -6 to 6
- out_cot: bfloat16 [256, 256, 128], P('row', 'col'), may hold values from -6 to 6
- tile_mask: int32 [2, 2], replicated, may hold values 0 or 1
- dilation: int32 [128], replicated, may hold values from 1 to 4, as said below
- norm_in_gain: float32 [128], replicated, may hold values from 0.5 to 1.5
- norm_in_bias: float32 [128], replicated, may hold values from -3 to 3
- proj_weight: bfloat16 [128, 256], replicated, may hold values from -0.5 to 0.5
- gate_weight: bfloat16 [128, 256], replicated, may hold values from -0.5 to 0.5
- norm_out_gain: float32 [128], replicated, may hold values from 0.5 to 1.5
- norm_out_bias: float32 [128], replicated, may hold values from -3 to 3
- out_weight: bfloat16 [128, 128], replicated, may hold values from -0.5 to 0.5
- out_gate_weight: bfloat16 [128, 128], replicated, may hold values from -0.5 to 0.5
- conv_weight: bfloat16 [9, 128, 128], replicated, may hold values from -0.1875 to 0.1875
Outputs:
- input_grad: bfloat16 [256, 256, 128], P('row', 'col')
- conv_weight_grad: float32 [9, 128, 128], replicated
Inputs may be any that keep to these rules, and one draw needn't show every extreme that they name: Some channel has dilation 4.
All inputs are finite; a program needn't handle non-finite values.
Results may differ from a plain program's by a relative error of at most 0.0065.
Values may be sent and summed in bfloat16 or wider, within the bound.
A program may use at most 64 MiB of HBM per device.

v0:
```python
import jax
import jax.numpy as jnp
from jax import lax
from jax.sharding import PartitionSpec as P

DILATION_LIMIT = 4


EPSILON = 1e-05


def extended(block, sides, width):
    for axis, dim in sides:
        count = lax.axis_size(axis)
        forward = [(i, i + 1) for i in range(count - 1)]
        backward = [(target, source) for source, target in forward]
        low = lax.ppermute(
            lax.slice_in_dim(block, block.shape[dim] - width, None, axis=dim), axis, forward
        )
        high = lax.ppermute(lax.slice_in_dim(block, 0, width, axis=dim), axis, backward)
        block = jnp.concatenate([low, block, high], axis=dim)
    return block


def layer_norm(value_entries, scale_gain, shift_bias, channel_axis):
    mean_value = jnp.mean(value_entries, axis=channel_axis, keepdims=True)
    centred = value_entries - mean_value
    variance = jnp.mean(centred * centred, axis=channel_axis, keepdims=True)
    inv_deviation = lax.rsqrt(variance + EPSILON)
    normed = centred * inv_deviation
    return (normed * scale_gain + shift_bias, normed, inv_deviation)


def norm_back(incoming, normed, inv_deviation, scale_gain, channel_axis):
    scaled = incoming * scale_gain
    mean_first = jnp.mean(scaled, axis=channel_axis, keepdims=True)
    second = jnp.mean(scaled * normed, axis=channel_axis, keepdims=True)
    return inv_deviation * (scaled - mean_first - normed * second)


def offsets():
    return [
        (row_stride, column_stride) for row_stride in (-1, 0, 1) for column_stride in (-1, 0, 1)
    ]


def on_device(
    convolution_input,
    pair,
    out_cot,
    tile_mask,
    dilation,
    norm_in_gain,
    norm_in_bias,
    proj_weight,
    gate_weight,
    norm_out_gain,
    norm_out_bias,
    out_weight,
    out_gate_weight,
    conv_weight,
):
    row_count, col_count, channels = pair.shape
    groups = lax.axis_size("row")
    total_rows = row_count * groups
    share_count = channels // groups
    row_start = lax.axis_index("row") * row_count
    col_start = lax.axis_index("col") * col_count
    tile_count = tile_mask.shape[0]
    tile_size = total_rows // tile_count
    tile_ids = jnp.arange(tile_count, dtype=jnp.int32)
    row_tiles = (row_start + jnp.arange(row_count, dtype=jnp.int32)) // tile_size
    col_tiles = (col_start + jnp.arange(col_count, dtype=jnp.int32)) // tile_size
    row_pick = (row_tiles[:, None] == tile_ids[None, :]).astype(jnp.float32)
    col_pick = (col_tiles[:, None] == tile_ids[None, :]).astype(jnp.float32)
    pair_mask = jnp.dot(jnp.dot(row_pick, tile_mask.astype(jnp.float32)), col_pick.T)
    in_gain = norm_in_gain[None, None, :]
    normed_in, in_hat, in_inv = layer_norm(
        pair.astype(jnp.float32), in_gain, norm_in_bias[None, None, :], 2
    )
    pair_norm = normed_in.astype(jnp.bfloat16)
    projected = jnp.einsum(
        "rkc,ce->erk", pair_norm, proj_weight, preferred_element_type=jnp.float32
    )
    gate_lin = jnp.einsum("rkc,ce->erk", pair_norm, gate_weight, preferred_element_type=jnp.float32)
    gate_sig = jax.nn.sigmoid(gate_lin)
    both_sides = (projected * gate_sig * pair_mask[None]).astype(jnp.bfloat16)
    split_sides = lax.all_to_all(
        both_sides.reshape(2, groups, share_count, row_count, col_count),
        "row",
        split_axis=1,
        concat_axis=3,
        tiled=True,
    )
    left_side = split_sides[0, 0]
    right_side = split_sides[1, 0]
    full_left, full_right = (
        lax.all_gather(left_side, "col", axis=2, tiled=True),
        lax.all_gather(right_side, "col", axis=2, tiled=True),
    )
    own_right = lax.dynamic_slice_in_dim(full_right, col_start, col_count, 1)
    product_split = jnp.einsum(
        "cik,cjk->cij", full_left, own_right, preferred_element_type=jnp.float32
    ).astype(jnp.bfloat16)
    product = lax.all_to_all(product_split, "row", split_axis=1, concat_axis=0, tiled=True)
    out_gain = norm_out_gain[:, None, None]
    normed_out, out_hat, out_inv = layer_norm(
        product.astype(jnp.float32), out_gain, norm_out_bias[:, None, None], 0
    )
    product_norm = normed_out.astype(jnp.bfloat16)
    out_lin = jnp.einsum(
        "crk,cd->rkd", product_norm, out_weight, preferred_element_type=jnp.float32
    )
    out_gate = jax.nn.sigmoid(
        jnp.einsum("rkc,cd->rkd", pair_norm, out_gate_weight, preferred_element_type=jnp.float32)
    )
    cotangent = out_cot.astype(jnp.float32)
    grad_lin = (cotangent * out_gate).astype(jnp.bfloat16)
    grad_gate = (cotangent * out_lin * out_gate * (1.0 - out_gate)).astype(jnp.bfloat16)
    grad_norm = jnp.einsum("rkd,cd->crk", grad_lin, out_weight, preferred_element_type=jnp.float32)
    grad_product = norm_back(grad_norm, out_hat, out_inv, out_gain, 0).astype(jnp.bfloat16)
    grad_split = lax.all_to_all(
        grad_product.reshape(groups, share_count, row_count, col_count),
        "row",
        split_axis=0,
        concat_axis=2,
        tiled=True,
    )[0]
    grad_full = lax.all_gather(grad_split, "col", axis=2, tiled=True)
    grad_left = jnp.einsum(
        "cij,cjk->cik", grad_full, right_side, preferred_element_type=jnp.float32
    )
    grad_right = jnp.einsum(
        "cij,cik->cjk", grad_full, left_side, preferred_element_type=jnp.float32
    )
    grad_pieces = jnp.stack([grad_left, grad_right]).astype(jnp.bfloat16)
    grad_back = lax.all_to_all(grad_pieces, "row", split_axis=2, concat_axis=1, tiled=True)
    grad_sides = (
        grad_back.reshape(2 * channels, row_count, col_count).astype(jnp.float32) * pair_mask[None]
    )
    grad_proj = (grad_sides * gate_sig).astype(jnp.bfloat16)
    grad_gatelin = (grad_sides * projected * gate_sig * (1.0 - gate_sig)).astype(jnp.bfloat16)
    grad_in = jnp.einsum("erk,ce->rkc", grad_proj, proj_weight, preferred_element_type=jnp.float32)
    grad_in = grad_in + jnp.einsum(
        "erk,ce->rkc", grad_gatelin, gate_weight, preferred_element_type=jnp.float32
    )
    grad_in = grad_in + jnp.einsum(
        "rkd,cd->rkc", grad_gate, out_gate_weight, preferred_element_type=jnp.float32
    )
    pair_gradient = (cotangent + norm_back(grad_in, in_hat, in_inv, in_gain, 2)).astype(
        jnp.bfloat16
    )
    bordered_input = extended(convolution_input, (("row", 0), ("col", 1)), DILATION_LIMIT)
    bordered_gradient = extended(pair_gradient, (("row", 0), ("col", 1)), DILATION_LIMIT)
    selected_entries = [dilation == shift_amount for shift_amount in range(1, DILATION_LIMIT + 1)]
    back_sum = pair_gradient.astype(jnp.float32)
    weight_terms = []
    for tap_index, (row_stride, column_stride) in enumerate(offsets()):
        tap_image = jnp.einsum(
            "pqo,io->pqi",
            bordered_gradient,
            conv_weight[tap_index],
            preferred_element_type=jnp.float32,
        )
        contribution = jnp.zeros(back_sum.shape, jnp.float32)
        shifted_input = jnp.zeros_like(convolution_input)
        for shift_amount in range(1, DILATION_LIMIT + 1):
            row_source = DILATION_LIMIT - shift_amount * row_stride
            column_source = DILATION_LIMIT - shift_amount * column_stride
            contribution = jnp.where(
                selected_entries[shift_amount - 1],
                tap_image[
                    row_source : row_source + row_count, column_source : column_source + col_count
                ],
                contribution,
            )
            row_inside = DILATION_LIMIT + shift_amount * row_stride
            column_inside = DILATION_LIMIT + shift_amount * column_stride
            shifted_input = jnp.where(
                selected_entries[shift_amount - 1],
                bordered_input[
                    row_inside : row_inside + row_count, column_inside : column_inside + col_count
                ],
                shifted_input,
            )
        back_sum = back_sum + contribution
        weight_terms.append(
            jnp.einsum(
                "pqi,pqo->io", shifted_input, pair_gradient, preferred_element_type=jnp.float32
            )
        )
    input_grad = back_sum.astype(jnp.bfloat16)
    weight_total = lax.psum(jnp.stack(weight_terms), ("row", "col"))
    return (input_grad, weight_total / total_rows)


def solution(mesh):
    placed = (
        P("row", "col", None),
        P("row", "col", None),
        P("row", "col", None),
        P(),
        P(),
        P(),
        P(),
        P(),
        P(),
        P(),
        P(),
        P(),
        P(),
        P(),
    )
    return jax.shard_map(
        on_device,
        mesh=mesh,
        in_specs=placed,
        out_specs=(P("row", "col", None), P()),
        check_vma=False,
    )
```

profile of v0, /device:TPU:0, one launch (start us, length us, event | category | flops | bytes accessed | tf_op | source)
XLA Modules:
  0.0 302.4 jit_solution(8528088319612465127)
XLA Ops:
  7.2 1.3 convert_reduce_fusion
  8.5 1.7 fusion.45
  11.2 2.2 fusion.254
  13.5 2.4 fusion.1
  16.7 33.3 %all_to_all.48 = bf16[2,32,4,8,256]{4,2,0,3,1:T(4,128)(2,1)S(1)} all-to-all(bf16[2,32,4,8,256]{4,2,0,3,1:T(4,128)(2,1)S(1)} %copy.37), channel_id=1, replica_groups=mesh['row'=32,'col'=1] {'row'}, dimensions={1} | all-to-all | bytes 2097152 | tf_op jit(solution)/shard_map/all_to_all | solution.py:88
  51.0 1.2 copy.40
  52.2 3.6 %all-to-all-start.1 = ((bf16[4,256,256]{2,0,1:T(4,128)(2,1)}), bf16[4,256,256]{2,0,1:T(4,128)(2,1)S(1)}, u32[]{:S(2)}, u32[]{:S(2)}) async-start(bf16[4,256,256]{2,0,1:T(4,128)(2,1)} %copy.40), calls=%async_computation.1 | async-start | bytes 1048576 | tf_op jit(solution)/shard_map/all_to_all | solution.py:105
  55.9 1.8 fusion.14
  57.7 13.8 %all-to-all-done.1 = bf16[4,256,256]{2,0,1:T(4,128)(2,1)S(1)} async-done(((bf16[4,256,256]{2,0,1:T(4,128)(2,1)}), bf16[4,256,256]{2,0,1:T(4,128)(2,1)S(1)}, u32[]{:S(2)}, u32[]{:S(2)}) %all-to-all-start.1) | async-done | bytes 524320 | tf_op jit(solution)/shard_map/all_to_all | solution.py:105
  72.6 1.6 reshape.106
  77.1 2.0 reshape.105
  79.1 1.3 copy.42
  80.4 18.4 %all_to_all.49 = bf16[32,4,8,256]{3,1,2,0:T(4,128)(2,1)S(1)} all-to-all(bf16[32,4,8,256]{3,1,2,0:T(4,128)(2,1)S(1)} %copy.42), channel_id=1, replica_groups=mesh['row'=32,'col'=1] {'row'}, dimensions={0} | all-to-all | bytes 1048576 | tf_op jit(solution)/shard_map/all_to_all | solution.py:122
  99.6 1.8 copy.45
  101.4 3.1 %all-to-all-start.3 = ((bf16[2,4,256,256]{3,1,0,2:T(4,128)(2,1)}), bf16[2,4,256,256]{3,1,0,2:T(4,128)(2,1)S(1)}, u32[]{:S(2)}, u32[]{:S(2)}) async-start(bf16[2,4,256,256]{3,1,0,2:T(4,128)(2,1)} %copy.45), calls=%async_computation.3 | async-start | bytes 2097152 | tf_op jit(solution)/shard_map/all_to_all | solution.py:137
  105.7 2.2 collective-permute-start.4
  107.8 1.3 collective-permute-start.5
  110.4 1.9 collective-permute-done.5
  115.7 3.1 %fusion.25 = f32[8,256,128]{2,1,0:T(8,128)} fusion(f32[8,256,128]{2,1,0:T(8,128)} %fusion.14, bf16[8,256,128]{2,1,0:T(8,128)(2,1)S(1)} %copy-done.5, f32[128,8,256]{2,0,1:T(8,128)S(1)} %reshape.106, f32[128]{0:T(128)S(1)} %copy-done.23, f32[128]{0:T(128)S(1)} %copy-done.21, f32[8,256]{1,0:T(8,128)S(1)} %broadcast_multiply_fusion.5, ...), kind=kOutput, calls=%fused_computation.66 | convolution fusion | flops 137101312 | bytes 3752960 | tf_op jit(solution)/shard_map/rkd,cd->rkc/dot_general | solution.py:147
  118.8 11.9 %all-to-all-done.3 = bf16[2,4,256,256]{3,1,0,2:T(4,128)(2,1)S(1)} async-done(((bf16[2,4,256,256]{3,1,0,2:T(4,128)(2,1)}), bf16[2,4,256,256]{3,1,0,2:T(4,128)(2,1)S(1)}, u32[]{:S(2)}, u32[]{:S(2)}) %all-to-all-start.3) | async-done | bytes 1048608 | tf_op jit(solution)/shard_map/all_to_all | solution.py:137
  130.7 1.9 copy_bitcast_fusion
  132.6 2.0 reshape.107
  134.7 2.2 fusion.49
  137.7 1.7 fusion.314
  139.4 1.3 fusion.47
  140.8 1.3 collective-permute-start.1
  142.1 3.0 %collective-permute-start = (bf16[4,256,128]{2,1,0:T(8,128)(2,1)S(1)}, bf16[4,256,128]{2,1,0:T(8,128)(2,1)S(1)}, u32[]{:S(2)}, u32[]{:S(2)}) collective-permute-start(bf16[4,256,128]{2,1,0:T(8,128)(2,1)S(1)} %get-tuple-element.17), channel_id=1, source_target_pairs={{0,1},{1,2},{2,3},{3,4},{4,5},{5,6},{6,7},{7,8},{8,9},{9,10},{10,1... | collective-permute-start | bytes 786440 | tf_op jit(solution)/shard_map/ppermute | solution.py:17
  150.3 2.2 fusion.29
  161.0 2.1 fusion.272
  163.1 7.1 %fusion.19 = bf16[8,256,128]{2,1,0:T(8,128)(2,1)} fusion(f32[16,264,128]{2,1,0:T(8,128)S(1)} %fusion.257, f32[16,264,128]{2,1,0:T(8,128)S(1)} %fusion.259, f32[16,264,128]{2,1,0:T(8,128)S(1)} %fusion.261, f32[16,264,128]{2,1,0:T(8,128)S(1)} %fusion.263, bf16[16,4,128]{2,1,0:T(4,128)(2,1)S(1)} %collective-permute-done.3, ...), kind=kOutput, calls=%fused_computation.60 | convolution fusion | flops 84672512 | bytes 35719168 | tf_op jit(solution)/shard_map/pqo,io->pqi/dot_general | solution.py:159
  170.2 123.4 %all-reduce.2.cloned.1.call-done = f32[9,128,128]{2,1,0:T(8,128)} async-done(((f32[9,128,128]{2,1,0:T(8,128)}), f32[9,128,128]{2,1,0:T(8,128)}) %all-reduce.2.cloned.1.call-update) | async-done | bytes 589840 | tf_op jit(solution)/shard_map/psum | solution.py:193
  293.7 1.9 broadcast_multiply_fusion
  (111 shorter events, 27.6 us)
Async XLA Ops:
  7.2 6.3 %copy-start = (bf16[128,256]{1,0:T(8,128)(2,1)S(1)}, bf16[128,256]{1,0:T(8,128)(2,1)}, u32[]{:S(2)}) copy-start(bf16[128,256]{1,0:T(8,128)(2,1)} %param.22) | copy-start | bytes 196612
  7.2 6.3 %copy-start.1 = (bf16[8,256,128]{2,1,0:T(8,128)(2,1)S(1)}, bf16[8,256,128]{2,1,0:T(8,128)(2,1)}, u32[]{:S(2)}) copy-start(bf16[8,256,128]{2,1,0:T(8,128)(2,1)} %param.15) | copy-start | bytes 1572868
  7.2 6.3 %copy-start.20 = (f32[128]{0:T(128)S(1)}, f32[128]{0:T(128)}, u32[]{:S(2)}) copy-start(f32[128]{0:T(128)} %param.19) | copy-start | bytes 1540
  7.2 6.3 %copy-start.22 = (f32[128]{0:T(128)S(1)}, f32[128]{0:T(128)}, u32[]{:S(2)}) copy-start(f32[128]{0:T(128)} %param.20) | copy-start | bytes 1540
  13.5 2.4 copy-start.2
  50.7 7.0 %copy-start.8 = (bf16[1,1,4,32,8,256]{5,2,0,4,3,1:T(4,128)(2,1)}, bf16[1,1,4,32,8,256]{5,2,0,4,3,1:T(4,128)(2,1)S(1)}, u32[]{:S(2)}) copy-start(bf16[1,1,4,32,8,256]{5,2,0,4,3,1:T(4,128)(2,1)S(1)} %get-tuple-element.10) | copy-start | bytes 1572868
  50.7 5.2 %copy-start.19 = (bf16[128,128]{1,0:T(8,128)(2,1)S(1)}, bf16[128,128]{1,0:T(8,128)(2,1)}, u32[]{:S(2)}) copy-start(bf16[128,128]{1,0:T(8,128)(2,1)} %param.26) | copy-start | bytes 98308
  52.2 19.2 %all-to-all-start.1 = ((bf16[4,256,256]{2,0,1:T(4,128)(2,1)}), bf16[4,256,256]{2,0,1:T(4,128)(2,1)S(1)}, u32[]{:S(2)}, u32[]{:S(2)}) async-start(bf16[4,256,256]{2,0,1:T(4,128)(2,1)} %copy.40), calls=%async_computation.1 | async-start | bytes 1048576 | tf_op jit(solution)/shard_map/all_to_all | solution.py:105
  74.2 1.4 copy-start.7
  74.2 1.4 copy-start.14
  74.2 1.4 copy-start.21
  77.1 21.8 %copy-start.9 = (bf16[1,1,4,32,8,256]{5,2,0,4,3,1:T(4,128)(2,1)S(1)}, bf16[1,1,4,32,8,256]{5,2,0,4,3,1:T(4,128)(2,1)}, u32[]{:S(2)}) copy-start(bf16[1,1,4,32,8,256]{5,2,0,4,3,1:T(4,128)(2,1)} %copy-done.8) | copy-start | bytes 1572868
  101.4 7.8 %copy-start.24 = (s32[128]{0:T(128)S(1)}, s32[128]{0:T(128)}, u32[]{:S(2)}) copy-start(s32[128]{0:T(128)} %param.18) | copy-start | bytes 1540
  101.4 29.3 %all-to-all-start.3 = ((bf16[2,4,256,256]{3,1,0,2:T(4,128)(2,1)}), bf16[2,4,256,256]{3,1,0,2:T(4,128)(2,1)S(1)}, u32[]{:S(2)}, u32[]{:S(2)}) async-start(bf16[2,4,256,256]{3,1,0,2:T(4,128)(2,1)} %copy.45), calls=%async_computation.3 | async-start | bytes 2097152 | tf_op jit(solution)/shard_map/all_to_all | solution.py:137
  104.5 189.2 %all-reduce.2.cloned.1.call-start = ((), (), s32[]{:S(2)}) async-start(), calls=%async_computation.4 | async-start | bytes 1179648 | tf_op jit(solution)/shard_map/psum | solution.py:193
  104.5 4.7 %copy-start.10 = (bf16[8,256,128]{2,1,0:T(8,128)(2,1)S(1)}, bf16[8,256,128]{2,1,0:T(8,128)(2,1)}, u32[]{:S(2)}) copy-start(bf16[8,256,128]{2,1,0:T(8,128)(2,1)} %param.14) | copy-start | bytes 1572868
  105.7 10.0 %copy-start.23 = (f32[128]{0:T(128)S(1)}, f32[128]{0:T(128)}, u32[]{:S(2)}) copy-start(f32[128]{0:T(128)} %param.24) | copy-start | bytes 1540
  105.7 3.5 %collective-permute-start.4 = (bf16[4,256,128]{2,1,0:T(8,128)(2,1)S(1)}, bf16[4,256,128]{2,1,0:T(8,128)(2,1)S(1)}, u32[]{:S(2)}, u32[]{:S(2)}) collective-permute-start(bf16[4,256,128]{2,1,0:T(8,128)(2,1)S(1)} %get-tuple-element.16), channel_id=1, source_target_pairs={{0,1},{1,2},{2,3},{3,4},{4,5},{5,6},{6,7},{7,8},{8,9},{9,10},{10,1... | collective-permute-start | bytes 786440 | tf_op jit(solution)/shard_map/ppermute | solution.py:17
  107.8 4.6 %collective-permute-start.5 = (bf16[4,256,128]{2,1,0:T(8,128)(2,1)S(1)}, bf16[4,256,128]{2,1,0:T(8,128)(2,1)S(1)}, u32[]{:S(2)}, u32[]{:S(2)}) collective-permute-start(bf16[4,256,128]{2,1,0:T(8,128)(2,1)S(1)} %get-tuple-element.15), channel_id=1, source_target_pairs={{1,0},{2,1},{3,2},{4,3},{5,4},{6,5},{7,6},{8,7},{9,8},{10,9},{11,1... | collective-permute-start | bytes 786440 | tf_op jit(solution)/shard_map/ppermute | solution.py:20
  110.4 2.7 copy-start.15
  114.2 31.0 %collective-permute-start.6 = (bf16[16,4,128]{2,1,0:T(4,128)(2,1)S(1)}, bf16[16,4,128]{2,1,0:T(4,128)(2,1)S(1)}, u32[]{:S(2)}, u32[]{:S(2)}) collective-permute-start(bf16[16,4,128]{2,1,0:T(4,128)(2,1)S(1)} %get-tuple-element.7), channel_id=1, source_target_pairs={} | collective-permute-start | bytes 49160 | tf_op jit(solution)/shard_map/ppermute | solution.py:17
  114.8 31.8 %collective-permute-start.7 = (bf16[16,4,128]{2,1,0:T(4,128)(2,1)S(1)}, bf16[16,4,128]{2,1,0:T(4,128)(2,1)S(1)}, u32[]{:S(2)}, u32[]{:S(2)}) collective-permute-start(bf16[16,4,128]{2,1,0:T(4,128)(2,1)S(1)} %get-tuple-element.6), channel_id=1, source_target_pairs={} | collective-permute-start | bytes 49160 | tf_op jit(solution)/shard_map/ppermute | solution.py:20
  132.6 2.0 copy-start.13
  134.6 2.3 copy-start.3
  134.6 2.8 copy-start.4
  134.6 3.1 %copy-start.6 = (f32[8,256,128]{2,1,0:T(8,128)S(1)}, f32[8,256,128]{2,1,0:T(8,128)}, u32[]{:S(2)}) copy-start(f32[8,256,128]{2,1,0:T(8,128)} %fusion.25) | copy-start | bytes 3145732
  139.4 5.7 %copy-start.18 = (bf16[16,256,128]{2,1,0:T(8,128)(2,1)S(1)}, bf16[16,256,128]{2,1,0:T(8,128)(2,1)}, u32[]{:S(2)}) copy-start(bf16[16,256,128]{2,1,0:T(8,128)(2,1)} %copy-done.17) | copy-start | bytes 3145732
  140.8 11.7 %collective-permute-start.1 = (bf16[4,256,128]{2,1,0:T(8,128)(2,1)S(1)}, bf16[4,256,128]{2,1,0:T(8,128)(2,1)S(1)}, u32[]{:S(2)}, u32[]{:S(2)}) collective-permute-start(bf16[4,256,128]{2,1,0:T(8,128)(2,1)S(1)} %get-tuple-element.18), channel_id=1, source_target_pairs={{1,0},{2,1},{3,2},{4,3},{5,4},{6,5},{7,6},{8,7},{9,8},{10,9},{11,1... | collective-permute-start | bytes 786440 | tf_op jit(solution)/shard_map/ppermute | solution.py:20
  142.1 10.4 %collective-permute-start = (bf16[4,256,128]{2,1,0:T(8,128)(2,1)S(1)}, bf16[4,256,128]{2,1,0:T(8,128)(2,1)S(1)}, u32[]{:S(2)}, u32[]{:S(2)}) collective-permute-start(bf16[4,256,128]{2,1,0:T(8,128)(2,1)S(1)} %get-tuple-element.17), channel_id=1, source_target_pairs={{0,1},{1,2},{2,3},{3,4},{4,5},{5,6},{6,7},{7,8},{8,9},{9,10},{10,1... | collective-permute-start | bytes 786440 | tf_op jit(solution)/shard_map/ppermute | solution.py:17
  152.5 3.3 %collective-permute-start.3 = (bf16[16,4,128]{2,1,0:T(4,128)(2,1)S(1)}, bf16[16,4,128]{2,1,0:T(4,128)(2,1)S(1)}, u32[]{:S(2)}, u32[]{:S(2)}) collective-permute-start(bf16[16,4,128]{2,1,0:T(4,128)(2,1)S(1)} %get-tuple-element.9), channel_id=1, source_target_pairs={} | collective-permute-start | bytes 49160 | tf_op jit(solution)/shard_map/ppermute | solution.py:20
  153.2 2.7 copy-start.25
  153.2 2.7 collective-permute-start.2
  (5 other events, 5.0 us)
Sparse Core Ops, SparseCore 0:
  155.9 137.6 all-reduce.1
where the time goes:
time: 303 us; the launch traced here: 302 us
  waiting for transfers between devices  151 us (50%)
  blocking collectives  51.8 us (17%)
  matrix products  37.4 us (12%)
  local copies, waits for them, and re-layouts  18.7 us (6%)
  starting transfers between devices  17.7 us (6%)
  between operations  14.8 us (5%)
  other arithmetic  11 us (4%)
    psum x1, waiting for transfers between devices, on_device(): weight_total = lax.psum(jnp.stack(weight_terms), ('row', 'col'))  123 us
    all_to_all x1, blocking collectives, on_device(): lax.all_to_all(both_sides.reshape(2, groups, share_count, row_count, col_...  33.3 us
    all_to_all x1, blocking collectives, on_device(): lax.all_to_all(grad_product.reshape(groups, share_count, row_count, col_c...  18.4 us
    dot_general x9, matrix products, on_device(): jnp.einsum('pqo,io->pqi', bordered_gradient, conv_weight[tap_index], pref...  14.3 us
    all_to_all x1, waiting for transfers between devices, on_device(): lax.all_to_all(product_split, 'row', split_axis=1, concat_axis=0, tiled=T...  13.8 us
    all_to_all x1, waiting for transfers between devices, on_device(): lax.all_to_all(grad_pieces, 'row', split_axis=2, concat_axis=1, tiled=True)  11.9 us
    dot_general x9, matrix products, on_device(): jnp.einsum('pqi,pqo->io', shifted_input, pair_gradient, preferred_element...  7.29 us
    ppermute x4, starting transfers between devices, extended(): lax.ppermute(lax.slice_in_dim(block, block.shape[dim] - width, None, axis...  6.88 us
  transfers between devices with their start and end apart: 11, of which 4 were waited for; matrix products, arithmetic and copies ran while one was open for 13% of the time, Pallas kernels for 0%

commit v1 on v0

--- a/solution.py
+++ b/solution.py
@@ -1,6 +1,10 @@
+import functools
+
 import jax
 import jax.numpy as jnp
 from jax import lax
+from jax.experimental import pallas as pl
+from jax.experimental.pallas import tpu as pltpu
 from jax.sharding import PartitionSpec as P
 
 DILATION_LIMIT = 4
@@ -42,6 +46,141 @@
     return [
         (row_stride, column_stride) for row_stride in (-1, 0, 1) for column_stride in (-1, 0, 1)
     ]
+
+
+def tap_weights(conv_weight, dilation):
+    by_tap = jnp.swapaxes(conv_weight, 1, 2)
+    blocks = []
+    for amount in range(1, DILATION_LIMIT + 1):
+        chosen = jnp.where(dilation == amount, by_tap, jnp.zeros((), by_tap.dtype))
+        for up in range(3):
+            blocks += [chosen[3 * up], chosen[3 * up + 2]]
+        blocks += [chosen[1], chosen[7]]
+    return jnp.concatenate(blocks + [by_tap[4]], axis=0)
+
+
+def conv_kernel(rows, cols, ext_ref, weight_ref, out_ref, wide_ref, sides_ref):
+    limit = DILATION_LIMIT
+    wide_ref[...] = ext_ref[...].astype(jnp.float32)
+    channels = ext_ref.shape[2]
+    for amount in range(1, limit + 1):
+        for side, sign in ((0, 1), (1, -1)):
+            sides_ref[amount - 1, :, :, side * channels : (side + 1) * channels] = wide_ref[
+                :, limit + sign * amount : limit + sign * amount + cols, :
+            ].astype(jnp.bfloat16)
+    sides_ref[limit, :, :, :channels] = wide_ref[:, limit : limit + cols, :].astype(jnp.bfloat16)
+
+    def one_row(row, carry):
+        base = row + limit
+        centre = sides_ref[limit, base, :, :channels]
+        size = 8 * channels
+        total = centre.astype(jnp.float32) + jnp.dot(
+            centre, weight_ref[limit * size : limit * size + channels, :], preferred_element_type=jnp.float32
+        )
+        for amount in range(1, limit + 1):
+            at = (amount - 1) * size
+            for up in range(3):
+                total += jnp.dot(
+                    sides_ref[amount - 1, base - amount * (up - 1)],
+                    weight_ref[at + 2 * up * channels : at + 2 * (up + 1) * channels, :],
+                    preferred_element_type=jnp.float32,
+                )
+            both = jnp.concatenate(
+                [
+                    sides_ref[limit, base + amount, :, :channels],
+                    sides_ref[limit, base - amount, :, :channels],
+                ],
+                axis=1,
+            )
+            total += jnp.dot(
+                both, weight_ref[at + 6 * channels : at + 8 * channels, :], preferred_element_type=jnp.float32
+            )
+        out_ref[row] = total.astype(out_ref.dtype)
+        return carry
+
+    lax.fori_loop(0, rows, one_row, 0)
+
+
+def conv_input_grad(bordered, weights, rows, cols):
+    channels = bordered.shape[2]
+    tall = bordered.shape[0]
+    return pl.pallas_call(
+        functools.partial(conv_kernel, rows, cols),
+        out_shape=jax.ShapeDtypeStruct((rows, cols, channels), jnp.bfloat16),
+        in_specs=[pl.BlockSpec(memory_space=pltpu.VMEM)] * 2,
+        out_specs=pl.BlockSpec(memory_space=pltpu.VMEM),
+        scratch_shapes=[
+            pltpu.VMEM(bordered.shape, jnp.float32),
+            pltpu.VMEM((DILATION_LIMIT + 1, tall, cols, 2 * channels), jnp.bfloat16),
+        ],
+        compiler_params=pltpu.CompilerParams(vmem_limit_bytes=32 * 2**20),
+        cost_estimate=pl.CostEstimate(
+            flops=2 * 33 * rows * cols * channels * channels, bytes_accessed=3 * 2**20, transcendentals=0
+        ),
+        name="conv_input_grad",
+    )(bordered, weights)
+
+
+def shift_kernel(rows, cols, ext_ref, dilation_ref, out_ref, wide_ref, picked_ref):
+    limit = DILATION_LIMIT
+    channels = ext_ref.shape[2]
+    wide_ref[...] = ext_ref[...].astype(jnp.float32)
+    dilation = dilation_ref[...]
+
+    def columns(row, carry):
+        for side in range(3):
+            picked = wide_ref[row, limit + side - 1 : limit + side - 1 + cols, :]
+            if side != 1:
+                for amount in range(2, limit + 1):
+                    start = limit + amount * (side - 1)
+                    picked = jnp.where(dilation == amount, wide_ref[row, start : start + cols, :], picked)
+            picked_ref[side, row] = picked
+        return carry
+
+    lax.fori_loop(0, rows + 2 * limit, columns, 0)
+
+    def one_row(row, carry):
+        base = row + limit
+        start = pl.multiple_of(row * cols, cols)
+        for up in range(3):
+            for side in range(3):
+                picked = picked_ref[side, base + up - 1]
+                if up != 1:
+                    for amount in range(2, limit + 1):
+                        picked = jnp.where(dilation == amount, picked_ref[side, base + amount * (up - 1)], picked)
+                tap = 3 * up + side
+                out_ref[pl.ds(start, cols), tap * channels : (tap + 1) * channels] = picked.astype(out_ref.dtype)
+        return carry
+
+    lax.fori_loop(0, rows, one_row, 0)
+
+
+def shifted_taps(bordered, dilation, rows, cols):
+    channels = bordered.shape[2]
+    return pl.pallas_call(
+        functools.partial(shift_kernel, rows, cols),
+        out_shape=jax.ShapeDtypeStruct((rows * cols, 9 * channels), jnp.bfloat16),
+        in_specs=[pl.BlockSpec(memory_space=pltpu.VMEM)] * 2,
+        out_specs=pl.BlockSpec(memory_space=pltpu.VMEM),
+        scratch_shapes=[
+            pltpu.VMEM(bordered.shape, jnp.float32),
+            pltpu.VMEM((3, bordered.shape[0], cols, channels), jnp.float32),
+        ],
+        compiler_params=pltpu.CompilerParams(vmem_limit_bytes=32 * 2**20),
+        cost_estimate=pl.CostEstimate(flops=10 * 2**20, bytes_accessed=6 * 2**20, transcendentals=0),
+        name="shifted_taps",
+    )(bordered, dilation[None, :])
+
+
+def summed(terms, groups):
+    rows, channels = terms.shape
+    parts = terms.astype(jnp.bfloat16).reshape(groups, rows // groups, channels)
+    parts = lax.all_to_all(parts, "row", split_axis=0, concat_axis=0, tiled=True)
+    part = jnp.sum(parts.astype(jnp.float32), axis=0)
+    if lax.axis_size("col") > 1:
+        part = lax.psum(part, "col")
+    spread = jnp.broadcast_to(part[None], (groups,) + part.shape)
+    return lax.all_to_all(spread, "row", split_axis=0, concat_axis=0, tiled=True).reshape(rows, channels)
 
 
 def on_device(
@@ -152,46 +291,16 @@
     )
     bordered_input = extended(convolution_input, (("row", 0), ("col", 1)), DILATION_LIMIT)
     bordered_gradient = extended(pair_gradient, (("row", 0), ("col", 1)), DILATION_LIMIT)
-    selected_entries = [dilation == shift_amount for shift_amount in range(1, DILATION_LIMIT + 1)]
-    back_sum = pair_gradient.astype(jnp.float32)
-    weight_terms = []
-    for tap_index, (row_stride, column_stride) in enumerate(offsets()):
-        tap_image = jnp.einsum(
-            "pqo,io->pqi",
-            bordered_gradient,
-            conv_weight[tap_index],
-            preferred_element_type=jnp.float32,
-        )
-        contribution = jnp.zeros(back_sum.shape, jnp.float32)
-        shifted_input = jnp.zeros_like(convolution_input)
-        for shift_amount in range(1, DILATION_LIMIT + 1):
-            row_source = DILATION_LIMIT - shift_amount * row_stride
-            column_source = DILATION_LIMIT - shift_amount * column_stride
-            contribution = jnp.where(
-                selected_entries[shift_amount - 1],
-                tap_image[
-                    row_source : row_source + row_count, column_source : column_source + col_count
-                ],
-                contribution,
-            )
-            row_inside = DILATION_LIMIT + shift_amount * row_stride
-            column_inside = DILATION_LIMIT + shift_amount * column_stride
-            shifted_input = jnp.where(
-                selected_entries[shift_amount - 1],
-                bordered_input[
-                    row_inside : row_inside + row_count, column_inside : column_inside + col_count
-                ],
-                shifted_input,
-            )
-        back_sum = back_sum + contribution
-        weight_terms.append(
-            jnp.einsum(
-                "pqi,pqo->io", shifted_input, pair_gradient, preferred_element_type=jnp.float32
-            )
-        )
-    input_grad = back_sum.astype(jnp.bfloat16)
-    weight_total = lax.psum(jnp.stack(weight_terms), ("row", "col"))
-    return (input_grad, weight_total / total_rows)
+    input_grad = conv_input_grad(bordered_gradient, tap_weights(conv_weight, dilation), row_count, col_count)
+    shifted_input = shifted_taps(bordered_input, dilation, row_count, col_count)
+    weight_terms = lax.dot_general(
+        shifted_input,
+        pair_gradient.reshape(row_count * col_count, channels),
+        (((0,), (0,)), ((), ())),
+        preferred_element_type=jnp.float32,
+    )
+    weight_total = summed(weight_terms, groups)
+    return (input_grad, weight_total.reshape(9, channels, channels) / total_rows)
 
 
 def solution(mesh):

time: 303 us -> 192 us (0.63)
  the two profiles are of different devices: /device:TPU:0 before, /device:TPU:16 now
where the time goes in v1:
time: 192 us; the launch traced here: 190 us
  waiting for transfers between devices  65.1 us (34%)
  starting transfers between devices  49.6 us (26%)
  local copies, waits for them, and re-layouts  31.8 us (17%)
  matrix products  20 us (10%)
  other arithmetic  11.9 us (6%)
  Pallas kernels  10.4 us (5%)
    unnamed x113, local copies, waits for them, and re-layouts  16.2 us
    all_to_all x1, waiting for transfers between devices, on_device(): lax.all_to_all(both_sides.reshape(2, groups, share_count, row_count, col_...  14.3 us
    ppermute x4, waiting for transfers between devices, extended(): lax.ppermute(lax.slice_in_dim(block, 0, width, axis=dim), axis, backward)  11.5 us
    ppermute x4, starting transfers between devices, extended(): lax.ppermute(lax.slice_in_dim(block, 0, width, axis=dim), axis, backward)  10.6 us
    all_to_all x1, waiting for transfers between devices, on_device(): lax.all_to_all(grad_product.reshape(groups, share_count, row_count, col_c...  9.42 us
    all_to_all x1, waiting for transfers between devices, summed(): lax.all_to_all(parts, 'row', split_axis=0, concat_axis=0, tiled=True)  9.18 us
    all_to_all x1, waiting for transfers between devices, on_device(): lax.all_to_all(product_split, 'row', split_axis=1, concat_axis=0, tiled=T...  9.14 us
    all_to_all x1, waiting for transfers between devices, on_device(): lax.all_to_all(grad_pieces, 'row', split_axis=2, concat_axis=1, tiled=True)  8.82 us
  transfers between devices with their start and end apart: 14, of which 7 were waited for; matrix products, arithmetic and copies ran while one was open for 17% of the time, Pallas kernels for 5%

profile of v1, /device:TPU:16, one launch (start us, length us, event | category | flops | bytes accessed | tf_op | source)
XLA Modules:
  0.0 190.4 jit_solution(17690717317770408)
XLA Ops:
  2.1 1.7 fusion.30
  4.2 1.7 fusion.65
  6.0 2.5 %fusion.1 = (bf16[256,8,256]{2,0,1:T(8,128)(2,1)S(1)}, f32[8,256,256]{1,2,0:T(8,128)}) fusion(f32[8,256,256]{1,2,0:T(8,128)S(1)} %fusion.65, f32[8,256]{1,0:T(8,128)S(1)} %fusion.22, bf16[128,256]{1,0:T(8,128)(2,1)S(1)} %copy-done, bf16[8,256,128]{2,1,0:T(8,128)(2,1)S(1)} %copy-done.3, f32[128]{0:T(128)S(1)} %copy-done.34, f32[128]{0:T(128)S(1)} %copy-done.31, ...), kind=kOutput, calls=%fused_computation.6 | convolution fusion | flops 138936320 | bytes 5858304 | tf_op jit(solution)/shard_map/rkc,ce->erk/dot_general | solution.py:224
  8.7 1.6 copy.40
  10.3 5.9 %all-to-all-start = ((bf16[2,32,4,8,256]{4,2,0,3,1:T(4,128)(2,1)}), bf16[2,32,4,8,256]{4,2,0,3,1:T(4,128)(2,1)S(1)}, u32[]{:S(2)}, u32[]{:S(2)}) async-start(bf16[2,32,4,8,256]{4,2,0,3,1:T(4,128)(2,1)} %copy.40), calls=%async_computation | async-start | bytes 2097152 | tf_op jit(solution)/shard_map/all_to_all | solution.py:227
  17.1 2.0 %collective-permute-start.4 = (bf16[4,256,128]{2,1,0:T(8,128)(2,1)}, bf16[4,256,128]{2,1,0:T(8,128)(2,1)}, u32[]{:S(2)}, u32[]{:S(2)}) collective-permute-start(bf16[4,256,128]{2,1,0:T(8,128)(2,1)} %get-tuple-element.13), channel_id=1, source_target_pairs={{0,1},{1,2},{2,3},{3,4},{4,5},{5,6},{6,7},{7,8},{8,9},{9,10},{10,1... | collective-permute-start | bytes 786440 | tf_op jit(solution)/shard_map/ppermute | solution.py:21
  19.1 5.3 %collective-permute-start.5 = (bf16[4,256,128]{2,1,0:T(8,128)(2,1)}, bf16[4,256,128]{2,1,0:T(8,128)(2,1)}, u32[]{:S(2)}, u32[]{:S(2)}) collective-permute-start(bf16[4,256,128]{2,1,0:T(8,128)(2,1)} %get-tuple-element.12), channel_id=1, source_target_pairs={{1,0},{2,1},{3,2},{4,3},{5,4},{6,5},{7,6},{8,7},{9,8},{10,9},{11,1... | collective-permute-start | bytes 786440 | tf_op jit(solution)/shard_map/ppermute | solution.py:24
  26.2 14.3 %all-to-all-done = bf16[2,32,4,8,256]{4,2,0,3,1:T(4,128)(2,1)S(1)} async-done(((bf16[2,32,4,8,256]{4,2,0,3,1:T(4,128)(2,1)}), bf16[2,32,4,8,256]{4,2,0,3,1:T(4,128)(2,1)S(1)}, u32[]{:S(2)}, u32[]{:S(2)}) %all-to-all-start) | async-done | bytes 1048608 | tf_op jit(solution)/shard_map/all_to_all | solution.py:227
  43.5 5.6 %all-to-all-start.1 = ((bf16[4,256,256]{2,0,1:T(4,128)(2,1)}), bf16[4,256,256]{2,0,1:T(4,128)(2,1)S(1)}, u32[]{:S(2)}, u32[]{:S(2)}) async-start(bf16[4,256,256]{2,0,1:T(4,128)(2,1)} %copy.43), calls=%async_computation.1 | async-start | bytes 1048576 | tf_op jit(solution)/shard_map/all_to_all | solution.py:244
  51.4 1.8 fusion.9
  53.2 9.1 %all-to-all-done.1 = bf16[4,256,256]{2,0,1:T(4,128)(2,1)S(1)} async-done(((bf16[4,256,256]{2,0,1:T(4,128)(2,1)}), bf16[4,256,256]{2,0,1:T(4,128)(2,1)S(1)}, u32[]{:S(2)}, u32[]{:S(2)}) %all-to-all-start.1) | async-done | bytes 524320 | tf_op jit(solution)/shard_map/all_to_all | solution.py:244
  63.5 1.6 reshape.117
  70.6 5.4 %all-to-all-start.2 = ((bf16[32,4,8,256]{3,1,2,0:T(4,128)(2,1)}), bf16[32,4,8,256]{3,1,2,0:T(4,128)(2,1)S(1)}, u32[]{:S(2)}, u32[]{:S(2)}) async-start(bf16[32,4,8,256]{3,1,2,0:T(4,128)(2,1)} %copy.45), calls=%async_computation.2 | async-start | bytes 1048576 | tf_op jit(solution)/shard_map/all_to_all | solution.py:261
  79.8 9.4 %all-to-all-done.2 = bf16[32,4,8,256]{3,1,2,0:T(4,128)(2,1)S(1)} async-done(((bf16[32,4,8,256]{3,1,2,0:T(4,128)(2,1)}), bf16[32,4,8,256]{3,1,2,0:T(4,128)(2,1)S(1)}, u32[]{:S(2)}, u32[]{:S(2)}) %all-to-all-start.2) | async-done | bytes 524320 | tf_op jit(solution)/shard_map/all_to_all | solution.py:261
  91.1 1.8 copy.48
  92.9 5.7 %all-to-all-start.3 = ((bf16[2,4,256,256]{3,1,0,2:T(4,128)(2,1)}), bf16[2,4,256,256]{3,1,0,2:T(4,128)(2,1)}, u32[]{:S(2)}, u32[]{:S(2)}) async-start(bf16[2,4,256,256]{3,1,0,2:T(4,128)(2,1)} %copy.48), calls=%async_computation.3 | async-start | bytes 2097152 | tf_op jit(solution)/shard_map/all_to_all | solution.py:276
  106.4 2.4 %shifted_taps.1 = bf16[2048,1152]{1,0:T(8,128)(2,1)S(1)} custom-call(bf16[16,264,128]{2,1,0:T(8,128)(2,1)S(1)} %pad_maximum_fusion.1.ext_ref, s32[1,128]{1,0:T(1,128)S(1)} %bitcast.250), custom_call_target="tpu_custom_call" | custom-call | flops 10485760 | bytes 6291456 | tf_op jit(solution)/shard_map/shifted_taps/pallas_call | solution.py:160
  108.8 2.1 %copy-done.1 = bf16[2048,1152]{1,0:T(8,128)(2,1)} copy-done((bf16[2048,1152]{1,0:T(8,128)(2,1)}, bf16[2048,1152]{1,0:T(8,128)(2,1)S(1)}, u32[]{:S(2)}) %copy-start.1) | copy-done | bytes 4718616
  110.9 3.1 %fusion.19 = f32[8,256,128]{2,1,0:T(8,128)} fusion(f32[8,256,128]{2,1,0:T(8,128)} %fusion.9, bf16[8,256,128]{2,1,0:T(8,128)(2,1)S(1)} %copy-done.6, f32[128,8,256]{2,0,1:T(8,128)S(1)} %reshape.117, f32[128]{0:T(128)S(1)} %copy-done.35, f32[128]{0:T(128)S(1)} %copy-done.33, f32[8,256]{1,0:T(8,128)S(1)} %broadcast_multiply_fusion.5, ...), kind=kOutput, calls=%fused_computation.38 | convolution fusion | flops 137101312 | bytes 3752960 | tf_op jit(solution)/shard_map/rkd,cd->rkc/dot_general | solution.py:286
  114.0 8.8 %all-to-all-done.3 = bf16[2,4,256,256]{3,1,0,2:T(4,128)(2,1)} async-done(((bf16[2,4,256,256]{3,1,0,2:T(4,128)(2,1)}), bf16[2,4,256,256]{3,1,0,2:T(4,128)(2,1)}, u32[]{:S(2)}, u32[]{:S(2)}) %all-to-all-start.3) | async-done | bytes 1048608 | tf_op jit(solution)/shard_map/all_to_all | solution.py:276
  122.8 3.1 %copy_bitcast_fusion = f32[2,32,4,8,256]{4,2,1,0,3:T(4,128)} fusion(bf16[2,4,32,8,256]{4,1,0,3,2:T(4,128)(2,1)} %bitcast.61), kind=kLoop, calls=%fused_computation.11 | loop fusion | flops 524288 | bytes 3145728 | tf_op jit(solution)/shard_map/convert_element_type | solution.py:278
  126.0 2.0 %reshape.118 = f32[256,8,256]{2,0,1:T(8,128)S(1)} reshape(f32[2,32,4,8,256]{4,2,1,0,3:T(4,128)} %copy_bitcast_fusion) | data formatting | bytes 4194304 | tf_op jit(solution)/shard_map/convert_element_type | solution.py:278
  128.0 2.3 %fusion.34 = f32[8,256,128]{2,1,0:T(8,128)S(1)} fusion(f32[8,256,256]{1,2,0:T(8,128)} %get-tuple-element.25, f32[256,8,256]{2,0,1:T(8,128)S(1)} %reshape.118, f32[8,256]{1,0:T(8,128)S(1)} %copy-done.30, bf16[128,256]{1,0:T(8,128)(2,1)} %param.21), kind=kOutput, calls=%fused_computation.53 | convolution fusion | flops 135790592 | bytes 5316608 | tf_op jit(solution)/shard_map/erk,ce->rkc/dot_general | solution.py:282
  130.4 4.4 %fusion.83 = (f32[8,256]{1,0:T(8,128)S(1)}, f32[8,256]{1,0:T(8,128)S(1)}, f32[8,256,128]{2,1,0:T(8,128)S(1)}) fusion(f32[8,256]{1,0:T(8,128)S(1)} %copy-done.26, f32[8,256]{1,0:T(8,128)S(1)} %copy-done.20, bf16[8,256,128]{2,1,0:T(8,128)(2,1)S(1)} %copy-done.4, f32[128]{0:T(128)S(1)} %copy-done.31, f32[8,256,128]{2,1,0:T(8,128)} %fusion.19, ...), kind=kOutput, calls=%fused_computation.197 | convolution fusion | flops 139718656 | bytes 10068480 | tf_op jit(solution)/shard_map/erk,ce->rkc/dot_general | solution.py:283
  138.3 5.6 %all-to-all-start.4 = ((bf16[32,36,128]{2,1,0:T(8,128)(2,1)}), bf16[32,36,128]{2,1,0:T(8,128)(2,1)S(1)}, u32[]{:S(2)}, u32[]{:S(2)}) async-start(bf16[32,36,128]{2,1,0:T(8,128)(2,1)} %reshape.116), calls=%async_computation.4 | async-start | bytes 655360 | tf_op jit(solution)/shard_map/all_to_all | solution.py:178
  144.0 9.2 %all-to-all-done.4 = bf16[32,36,128]{2,1,0:T(8,128)(2,1)S(1)} async-done(((bf16[32,36,128]{2,1,0:T(8,128)(2,1)}), bf16[32,36,128]{2,1,0:T(8,128)(2,1)S(1)}, u32[]{:S(2)}, u32[]{:S(2)}) %all-to-all-start.4) | async-done | bytes 294944 | tf_op jit(solution)/shard_map/all_to_all | solution.py:178
  154.1 5.3 %all-to-all-start.5 = ((f32[32,36,128]{2,1,0:T(8,128)}), f32[32,36,128]{2,1,0:T(8,128)S(1)}, u32[]{:S(2)}, u32[]{:S(2)}) async-start(f32[32,36,128]{2,1,0:T(8,128)} %broadcast_in_dim.53), calls=%async_computation.5 | async-start | bytes 1310720 | tf_op jit(solution)/shard_map/all_to_all | solution.py:183
  159.5 4.0 %collective-permute-start.1 = (bf16[4,256,128]{2,1,0:T(8,128)(2,1)S(1)}, bf16[4,256,128]{2,1,0:T(8,128)(2,1)S(1)}, u32[]{:S(2)}, u32[]{:S(2)}) collective-permute-start(bf16[4,256,128]{2,1,0:T(8,128)(2,1)S(1)} %get-tuple-element.15), channel_id=1, source_target_pairs={{1,0},{2,1},{3,2},{4,3},{5,4},{6,5},{7,6},{8,7},{9,8},{10,9},{11,1... | collective-permute-start | bytes 786440 | tf_op jit(solution)/shard_map/ppermute | solution.py:24
  163.5 1.9 %collective-permute-start = (bf16[4,256,128]{2,1,0:T(8,128)(2,1)S(1)}, bf16[4,256,128]{2,1,0:T(8,128)(2,1)S(1)}, u32[]{:S(2)}, u32[]{:S(2)}) collective-permute-start(bf16[4,256,128]{2,1,0:T(8,128)(2,1)S(1)} %get-tuple-element.14), channel_id=1, source_target_pairs={{0,1},{1,2},{2,3},{3,4},{4,5},{5,6},{6,7},{7,8},{8,9},{9,10},{10,1... | collective-permute-start | bytes 786440 | tf_op jit(solution)/shard_map/ppermute | solution.py:21
  165.5 11.5 %collective-permute-done.1 = bf16[4,256,128]{2,1,0:T(8,128)(2,1)S(1)} collective-permute-done((bf16[4,256,128]{2,1,0:T(8,128)(2,1)S(1)}, bf16[4,256,128]{2,1,0:T(8,128)(2,1)S(1)}, u32[]{:S(2)}, u32[]{:S(2)}) %collective-permute-start.1) | collective-permute-done | bytes 262176 | tf_op jit(solution)/shard_map/ppermute | solution.py:24
  177.0 2.7 %collective-permute-done = bf16[4,256,128]{2,1,0:T(8,128)(2,1)S(1)} collective-permute-done((bf16[4,256,128]{2,1,0:T(8,128)(2,1)S(1)}, bf16[4,256,128]{2,1,0:T(8,128)(2,1)S(1)}, u32[]{:S(2)}, u32[]{:S(2)}) %collective-permute-start) | collective-permute-done | bytes 262176 | tf_op jit(solution)/shard_map/ppermute | solution.py:21
  181.4 8.1 %conv_input_grad.1 = bf16[8,256,128]{2,1,0:T(8,128)(2,1)} custom-call(bf16[16,264,128]{2,1,0:T(8,128)(2,1)S(1)} %pad_maximum_fusion.ext_ref, bf16[4224,128]{1,0:T(8,128)(2,1)S(1)} %constant_dynamic-update-slice_fusion.weight_ref), custom_call_target="tpu_custom_call" | custom-call | flops 2214592512 | bytes 3145728 | tf_op jit(solution)/shard_map/conv_input_grad/pallas_call | solution.py:107
  (167 shorter events, 36.9 us)
Async XLA Ops:
  0.6 5.3 %copy-start = (bf16[128,256]{1,0:T(8,128)(2,1)S(1)}, bf16[128,256]{1,0:T(8,128)(2,1)}, u32[]{:S(2)}) copy-start(bf16[128,256]{1,0:T(8,128)(2,1)} %param.22) | copy-start | bytes 196612
  2.1 49.3 %copy-start.19 = (f32[8,256]{1,0:T(8,128)}, f32[8,256]{1,0:T(8,128)S(1)}, u32[]{:S(2)}) copy-start(f32[8,256]{1,0:T(8,128)S(1)} %broadcast_multiply_fusion.6) | copy-start | bytes 24580
  3.8 47.6 %copy-start.25 = (f32[8,256]{1,0:T(8,128)}, f32[8,256]{1,0:T(8,128)S(1)}, u32[]{:S(2)}) copy-start(f32[8,256]{1,0:T(8,128)S(1)} %add_rsqrt_fusion.1) | copy-start | bytes 24580
  10.3 6.0 %copy-start.9 = (bf16[8,256,128]{2,1,0:T(8,128)(2,1)S(1)}, bf16[8,256,128]{2,1,0:T(8,128)(2,1)}, u32[]{:S(2)}) copy-start(bf16[8,256,128]{2,1,0:T(8,128)(2,1)} %param.14) | copy-start | bytes 1572868
  10.3 14.2 %copy-start.2 = (s32[128]{0:T(128)S(1)}, s32[128]{0:T(128)}, u32[]{:S(2)}) copy-start(s32[128]{0:T(128)} %param.18) | copy-start | bytes 1540
  10.3 14.2 %copy-start.17 = (bf16[9,128,128]{2,1,0:T(8,128)(2,1)S(1)}, bf16[9,128,128]{2,1,0:T(8,128)(2,1)}, u32[]{:S(2)}) copy-start(bf16[9,128,128]{2,1,0:T(8,128)(2,1)} %param.27) | copy-start | bytes 884740
  10.3 30.3 %all-to-all-start = ((bf16[2,32,4,8,256]{4,2,0,3,1:T(4,128)(2,1)}), bf16[2,32,4,8,256]{4,2,0,3,1:T(4,128)(2,1)S(1)}, u32[]{:S(2)}, u32[]{:S(2)}) async-start(bf16[2,32,4,8,256]{4,2,0,3,1:T(4,128)(2,1)} %copy.40), calls=%async_computation | async-start | bytes 2097152 | tf_op jit(solution)/shard_map/all_to_all | solution.py:227
  17.1 84.6 %collective-permute-start.4 = (bf16[4,256,128]{2,1,0:T(8,128)(2,1)}, bf16[4,256,128]{2,1,0:T(8,128)(2,1)}, u32[]{:S(2)}, u32[]{:S(2)}) collective-permute-start(bf16[4,256,128]{2,1,0:T(8,128)(2,1)} %get-tuple-element.13), channel_id=1, source_target_pairs={{0,1},{1,2},{2,3},{3,4},{4,5},{5,6},{6,7},{7,8},{8,9},{9,10},{10,1... | collective-permute-start | bytes 786440 | tf_op jit(solution)/shard_map/ppermute | solution.py:21
  19.1 83.6 %collective-permute-start.5 = (bf16[4,256,128]{2,1,0:T(8,128)(2,1)}, bf16[4,256,128]{2,1,0:T(8,128)(2,1)}, u32[]{:S(2)}, u32[]{:S(2)}) collective-permute-start(bf16[4,256,128]{2,1,0:T(8,128)(2,1)} %get-tuple-element.12), channel_id=1, source_target_pairs={{1,0},{2,1},{3,2},{4,3},{5,4},{6,5},{7,6},{8,7},{9,8},{10,9},{11,1... | collective-permute-start | bytes 786440 | tf_op jit(solution)/shard_map/ppermute | solution.py:24
  25.5 25.9 %copy-start.15 = (bf16[9,128,128]{2,1,0:T(8,128)(2,1)}, bf16[9,128,128]{2,1,0:T(8,128)(2,1)S(1)}, u32[]{:S(2)}) copy-start(bf16[9,128,128]{2,1,0:T(8,128)(2,1)S(1)} %get-tuple-element.19) | copy-start | bytes 884740
  42.3 9.1 %copy-start.27 = (bf16[128,128]{1,0:T(8,128)(2,1)S(1)}, bf16[128,128]{1,0:T(8,128)(2,1)}, u32[]{:S(2)}) copy-start(bf16[128,128]{1,0:T(8,128)(2,1)} %param.26) | copy-start | bytes 98308
  43.5 18.8 %all-to-all-start.1 = ((bf16[4,256,256]{2,0,1:T(4,128)(2,1)}), bf16[4,256,256]{2,0,1:T(4,128)(2,1)S(1)}, u32[]{:S(2)}, u32[]{:S(2)}) async-start(bf16[4,256,256]{2,0,1:T(4,128)(2,1)} %copy.43), calls=%async_computation.1 | async-start | bytes 1048576 | tf_op jit(solution)/shard_map/all_to_all | solution.py:244
  70.6 18.6 %all-to-all-start.2 = ((bf16[32,4,8,256]{3,1,2,0:T(4,128)(2,1)}), bf16[32,4,8,256]{3,1,2,0:T(4,128)(2,1)S(1)}, u32[]{:S(2)}, u32[]{:S(2)}) async-start(bf16[32,4,8,256]{3,1,2,0:T(4,128)(2,1)} %copy.45), calls=%async_computation.2 | async-start | bytes 1048576 | tf_op jit(solution)/shard_map/all_to_all | solution.py:261
  92.9 9.8 %copy-start.10 = (bf16[8,256,128]{2,1,0:T(8,128)(2,1)S(1)}, bf16[8,256,128]{2,1,0:T(8,128)(2,1)}, u32[]{:S(2)}) copy-start(bf16[8,256,128]{2,1,0:T(8,128)(2,1)} %param.14) | copy-start | bytes 1572868
  92.9 30.0 %all-to-all-start.3 = ((bf16[2,4,256,256]{3,1,0,2:T(4,128)(2,1)}), bf16[2,4,256,256]{3,1,0,2:T(4,128)(2,1)}, u32[]{:S(2)}, u32[]{:S(2)}) async-start(bf16[2,4,256,256]{3,1,0,2:T(4,128)(2,1)} %copy.48), calls=%async_computation.3 | async-start | bytes 2097152 | tf_op jit(solution)/shard_map/all_to_all | solution.py:276
  103.8 2.3 %collective-permute-start.7 = (bf16[16,4,128]{2,1,0:T(4,128)(2,1)S(1)}, bf16[16,4,128]{2,1,0:T(4,128)(2,1)S(1)}, u32[]{:S(2)}, u32[]{:S(2)}) collective-permute-start(bf16[16,4,128]{2,1,0:T(4,128)(2,1)S(1)} %get-tuple-element.7), channel_id=1, source_target_pairs={} | collective-permute-start | bytes 49160 | tf_op jit(solution)/shard_map/ppermute | solution.py:24
  104.4 1.6 collective-permute-start.6
  106.3 4.6 %copy-start.22 = (bf16[128,128]{1,0:T(8,128)(2,1)S(1)}, bf16[128,128]{1,0:T(8,128)(2,1)}, u32[]{:S(2)}) copy-start(bf16[128,128]{1,0:T(8,128)(2,1)} %param.25) | copy-start | bytes 98308
  106.4 4.6 %copy-start.24 = (f32[8,256]{1,0:T(8,128)S(1)}, f32[8,256]{1,0:T(8,128)}, u32[]{:S(2)}) copy-start(f32[8,256]{1,0:T(8,128)} %copy-done.23) | copy-start | bytes 24580
  106.4 4.6 %copy-start.28 = (bf16[128,128]{1,0:T(8,128)(2,1)S(1)}, bf16[128,128]{1,0:T(8,128)(2,1)}, u32[]{:S(2)}) copy-start(bf16[128,128]{1,0:T(8,128)(2,1)} %param.26) | copy-start | bytes 98308
  106.4 4.5 %copy-start.33 = (f32[128]{0:T(128)S(1)}, f32[128]{0:T(128)}, u32[]{:S(2)}) copy-start(f32[128]{0:T(128)} %param.23) | copy-start | bytes 1540
  106.4 4.5 %copy-start.35 = (f32[128]{0:T(128)S(1)}, f32[128]{0:T(128)}, u32[]{:S(2)}) copy-start(f32[128]{0:T(128)} %param.24) | copy-start | bytes 1540
  128.0 8.1 %slice-start = ((s8[4718592]{0:T(1024)(128)(4,1)}), s8[4194304]{0:T(1024)(128)(4,1)S(1)}, s32[]{:S(2)}) async-start(s8[4718592]{0:T(1024)(128)(4,1)} %bitcast.248), calls=%async_computation.6 | async-start | bytes 8388608
  130.4 4.4 %copy-start.7 = (bf16[8,256,128]{2,1,0:T(8,128)(2,1)S(1)}, bf16[8,256,128]{2,1,0:T(8,128)(2,1)}, u32[]{:S(2)}) copy-start(bf16[8,256,128]{2,1,0:T(8,128)(2,1)} %param.16) | copy-start | bytes 1572868
  130.4 5.7 %slice-start.1 = ((s8[4718592]{0:T(1024)(128)(4,1)}), s8[524288]{0:T(1024)(128)(4,1)S(1)}, s32[]{:S(2)}) async-start(s8[4718592]{0:T(1024)(128)(4,1)} %bitcast.248), calls=%async_computation.7 | async-start | bytes 1048576
  137.5 6.4 %copy-start.14 = (bf16[9,128,128]{2,1,0:T(8,128)(2,1)S(1)}, bf16[9,128,128]{2,1,0:T(8,128)(2,1)}, u32[]{:S(2)}) copy-start(bf16[9,128,128]{2,1,0:T(8,128)(2,1)} %get-tuple-element.16) | copy-start | bytes 884740
  138.3 14.8 %all-to-all-start.4 = ((bf16[32,36,128]{2,1,0:T(8,128)(2,1)}), bf16[32,36,128]{2,1,0:T(8,128)(2,1)S(1)}, u32[]{:S(2)}, u32[]{:S(2)}) async-start(bf16[32,36,128]{2,1,0:T(8,128)(2,1)} %reshape.116), calls=%async_computation.4 | async-start | bytes 655360 | tf_op jit(solution)/shard_map/all_to_all | solution.py:178
  154.1 35.4 %all-to-all-start.5 = ((f32[32,36,128]{2,1,0:T(8,128)}), f32[32,36,128]{2,1,0:T(8,128)S(1)}, u32[]{:S(2)}, u32[]{:S(2)}) async-start(f32[32,36,128]{2,1,0:T(8,128)} %broadcast_in_dim.53), calls=%async_computation.5 | async-start | bytes 1310720 | tf_op jit(solution)/shard_map/all_to_all | solution.py:183
  159.5 17.4 %collective-permute-start.1 = (bf16[4,256,128]{2,1,0:T(8,128)(2,1)S(1)}, bf16[4,256,128]{2,1,0:T(8,128)(2,1)S(1)}, u32[]{:S(2)}, u32[]{:S(2)}) collective-permute-start(bf16[4,256,128]{2,1,0:T(8,128)(2,1)S(1)} %get-tuple-element.15), channel_id=1, source_target_pairs={{1,0},{2,1},{3,2},{4,3},{5,4},{6,5},{7,6},{8,7},{9,8},{10,9},{11,1... | collective-permute-start | bytes 786440 | tf_op jit(solution)/shard_map/ppermute | solution.py:24
  163.5 16.2 %collective-permute-start = (bf16[4,256,128]{2,1,0:T(8,128)(2,1)S(1)}, bf16[4,256,128]{2,1,0:T(8,128)(2,1)S(1)}, u32[]{:S(2)}, u32[]{:S(2)}) collective-permute-start(bf16[4,256,128]{2,1,0:T(8,128)(2,1)S(1)} %get-tuple-element.14), channel_id=1, source_target_pairs={{0,1},{1,2},{2,3},{3,4},{4,5},{5,6},{6,7},{7,8},{8,9},{9,10},{10,1... | collective-permute-start | bytes 786440 | tf_op jit(solution)/shard_map/ppermute | solution.py:21
  179.7 1.3 collective-permute-start.3
  180.4 0.7 collective-permute-start.2
  (21 other events, 42.6 us)

commit v2 on v1

--- a/solution.py
+++ b/solution.py
@@ -46,6 +46,150 @@
     return [
         (row_stride, column_stride) for row_stride in (-1, 0, 1) for column_stride in (-1, 0, 1)
     ]
+
+
+def greet(groups):
+    me = lax.axis_index("row")
+    barrier = pltpu.get_barrier_semaphore()
+
+    def one(step, carry):
+        peer = lax.rem(me + step, groups)
+        pl.semaphore_signal(barrier, inc=1, device_id={"row": peer}, device_id_type=pl.DeviceIdType.MESH)
+        return carry
+
+    lax.fori_loop(1, groups, one, 0)
+    pl.semaphore_wait(barrier, groups - 1)
+    return me
+
+
+def piece(me, source_ref, landed_ref, send_sem, recv_sem, peer):
+    return pltpu.make_async_remote_copy(
+        src_ref=source_ref.at[peer],
+        dst_ref=landed_ref.at[me],
+        send_sem=send_sem.at[peer],
+        recv_sem=recv_sem.at[me],
+        device_id={"row": peer},
+        device_id_type=pl.DeviceIdType.MESH,
+    )
+
+
+def send_all(groups, me, source_ref, landed_ref, send_sem, recv_sem):
+    def one(step, carry):
+        piece(me, source_ref, landed_ref, send_sem, recv_sem, lax.rem(me + step, groups)).start()
+        return carry
+
+    lax.fori_loop(1, groups, one, 0)
+    landed_ref[me] = source_ref[me]
+
+
+def wait_all(groups, me, source_ref, landed_ref, send_sem, recv_sem):
+    def one(step, carry):
+        peer = lax.rem(me + groups - step, groups)
+        pltpu.make_async_remote_copy(
+            src_ref=source_ref.at[peer],
+            dst_ref=landed_ref.at[peer],
+            send_sem=send_sem.at[peer],
+            recv_sem=recv_sem.at[peer],
+            device_id={"row": peer},
+            device_id_type=pl.DeviceIdType.MESH,
+        ).wait()
+        return carry
+
+    lax.fori_loop(1, groups, one, 0)
+
+
+def product_kernel(groups, share, rows, cols, source_ref, product_ref, sides_ref, landed, staged, *sems):
+    me = greet(groups)
+    send_all(groups, me, source_ref, landed, sems[0], sems[1])
+    wait_all(groups, me, source_ref, landed, sems[0], sems[1])
+    total = groups * rows
+    for pair in range(share // 2):
+        results = []
+        for channel in (2 * pair, 2 * pair + 1):
+            both = landed[:, channel].astype(jnp.float32)
+            left = both[:, :rows].reshape(total, cols).astype(jnp.bfloat16)
+            right = both[:, rows:].reshape(total, cols).astype(jnp.bfloat16)
+            sides_ref[channel, 0] = left
+            sides_ref[channel, 1] = right
+            product = lax.dot_general(
+                left, right, (((1,), (1,)), ((), ())), preferred_element_type=jnp.float32
+            )
+            results.append(product.reshape(groups, rows, total))
+        staged[:, 2 * pair * rows : 2 * (pair + 1) * rows, :] = jnp.concatenate(results, axis=1).astype(
+            jnp.bfloat16
+        )
+    send_all(groups, me, staged, product_ref, sems[2], sems[3])
+    wait_all(groups, me, staged, product_ref, sems[2], sems[3])
+
+
+def back_kernel(groups, share, rows, cols, source_ref, sides_ref, grads_ref, landed, staged, *sems):
+    me = greet(groups)
+    send_all(groups, me, source_ref, landed, sems[0], sems[1])
+    wait_all(groups, me, source_ref, landed, sems[0], sems[1])
+    total = groups * rows
+    for pair in range(share // 2):
+        both = landed[:, 2 * pair * rows : 2 * (pair + 1) * rows, :].astype(jnp.float32)
+        for part in range(2):
+            channel = 2 * pair + part
+            incoming = both[:, part * rows : (part + 1) * rows].reshape(total, cols).astype(jnp.bfloat16)
+            grad_left = jnp.dot(incoming, sides_ref[channel, 1], preferred_element_type=jnp.float32)
+            grad_right = lax.dot_general(
+                incoming, sides_ref[channel, 0], (((0,), (0,)), ((), ())), preferred_element_type=jnp.float32
+            )
+            staged[:, channel] = jnp.concatenate(
+                [grad_left.reshape(groups, rows, cols), grad_right.reshape(groups, rows, cols)], axis=1
+            ).astype(jnp.bfloat16)
+    send_all(groups, me, staged, grads_ref, sems[2], sems[3])
+    wait_all(groups, me, staged, grads_ref, sems[2], sems[3])
+
+
+def triangle_product(source):
+    groups, share, two_rows, cols = source.shape
+    rows = two_rows // 2
+    vmem = pl.BlockSpec(memory_space=pltpu.VMEM)
+    return pl.pallas_call(
+        functools.partial(product_kernel, groups, share, rows, cols),
+        out_shape=(
+            jax.ShapeDtypeStruct((groups, share * rows, cols), jnp.bfloat16),
+            jax.ShapeDtypeStruct((share, 2, groups * rows, cols), jnp.bfloat16),
+        ),
+        in_specs=[vmem],
+        out_specs=(vmem, vmem),
+        scratch_shapes=[
+            pltpu.VMEM(source.shape, jnp.bfloat16),
+            pltpu.VMEM((groups, share * rows, cols), jnp.bfloat16),
+        ]
+        + [pltpu.SemaphoreType.DMA((groups,))] * 4,
+        compiler_params=pltpu.CompilerParams(
+            vmem_limit_bytes=32 * 2**20, collective_id=0, has_side_effects=True
+        ),
+        name="triangle_product",
+    )(source)
+
+
+def triangle_back(source, sides):
+    groups, deep, cols = source.shape
+    share = sides.shape[0]
+    rows = deep // share
+    vmem = pl.BlockSpec(memory_space=pltpu.VMEM)
+    shape = (groups, share, 2 * rows, cols)
+    return pl.pallas_call(
+        functools.partial(back_kernel, groups, share, rows, cols),
+        out_shape=jax.ShapeDtypeStruct(shape, jnp.bfloat16),
+        in_specs=[vmem, vmem],
+        out_specs=vmem,
+        scratch_shapes=[pltpu.VMEM(source.shape, jnp.bfloat16), pltpu.VMEM(shape, jnp.bfloat16)]
+        + [pltpu.SemaphoreType.DMA((groups,))] * 4,
+        compiler_params=pltpu.CompilerParams(
+            vmem_limit_bytes=32 * 2**20, collective_id=1, has_side_effects=True
+        ),
+        name="triangle_back",
+    )(source, sides)
+
+
+def interleaved(weight):
+    depth, wide = weight.shape
+    return jnp.swapaxes(weight.reshape(depth, 2, wide // 2), 1, 2).reshape(depth, wide)
 
 
 def tap_weights(conv_weight, dilation):
@@ -213,6 +357,9 @@
     row_pick = (row_tiles[:, None] == tile_ids[None, :]).astype(jnp.float32)
     col_pick = (col_tiles[:, None] == tile_ids[None, :]).astype(jnp.float32)
     pair_mask = jnp.dot(jnp.dot(row_pick, tile_mask.astype(jnp.float32)), col_pick.T)
+    whole_cols = lax.axis_size("col") == 1 and row_count % 8 == 0 and share_count % 2 == 0
+    if whole_cols:
+        proj_weight, gate_weight = interleaved(proj_weight), interleaved(gate_weight)
     in_gain = norm_in_gain[None, None, :]
     normed_in, in_hat, in_inv = layer_norm(
         pair.astype(jnp.float32), in_gain, norm_in_bias[None, None, :], 2
@@ -224,24 +371,30 @@
     gate_lin = jnp.einsum("rkc,ce->erk", pair_norm, gate_weight, preferred_element_type=jnp.float32)
     gate_sig = jax.nn.sigmoid(gate_lin)
     both_sides = (projected * gate_sig * pair_mask[None]).astype(jnp.bfloat16)
-    split_sides = lax.all_to_all(
-        both_sides.reshape(2, groups, share_count, row_count, col_count),
-        "row",
-        split_axis=1,
-        concat_axis=3,
-        tiled=True,
-    )
-    left_side = split_sides[0, 0]
-    right_side = split_sides[1, 0]
-    full_left, full_right = (
-        lax.all_gather(left_side, "col", axis=2, tiled=True),
-        lax.all_gather(right_side, "col", axis=2, tiled=True),
-    )
-    own_right = lax.dynamic_slice_in_dim(full_right, col_start, col_count, 1)
-    product_split = jnp.einsum(
-        "cik,cjk->cij", full_left, own_right, preferred_element_type=jnp.float32
-    ).astype(jnp.bfloat16)
-    product = lax.all_to_all(product_split, "row", split_axis=1, concat_axis=0, tiled=True)
+    if whole_cols:
+        product, own_sides = triangle_product(
+            both_sides.reshape(groups, share_count, 2 * row_count, col_count)
+        )
+        product = product.reshape(channels, row_count, col_count)
+    else:
+        split_sides = lax.all_to_all(
+            both_sides.reshape(2, groups, share_count, row_count, col_count),
+            "row",
+            split_axis=1,
+            concat_axis=3,
+            tiled=True,
+        )
+        left_side = split_sides[0, 0]
+        right_side = split_sides[1, 0]
+        full_left, full_right = (
+            lax.all_gather(left_side, "col", axis=2, tiled=True),
+            lax.all_gather(right_side, "col", axis=2, tiled=True),
+        )
+        own_right = lax.dynamic_slice_in_dim(full_right, col_start, col_count, 1)
+        product_split = jnp.einsum(
+            "cik,cjk->cij", full_left, own_right, preferred_element_type=jnp.float32
+        ).astype(jnp.bfloat16)
+        product = lax.all_to_all(product_split, "row", split_axis=1, concat_axis=0, tiled=True)
     out_gain = norm_out_gain[:, None, None]
     normed_out, out_hat, out_inv = layer_norm(
         product.astype(jnp.float32), out_gain, norm_out_bias[:, None, None], 0
@@ -258,22 +411,27 @@
     grad_gate = (cotangent * out_lin * out_gate * (1.0 - out_gate)).astype(jnp.bfloat16)
     grad_norm = jnp.einsum("rkd,cd->crk", grad_lin, out_weight, preferred_element_type=jnp.float32)
     grad_product = norm_back(grad_norm, out_hat, out_inv, out_gain, 0).astype(jnp.bfloat16)
-    grad_split = lax.all_to_all(
-        grad_product.reshape(groups, share_count, row_count, col_count),
-        "row",
-        split_axis=0,
-        concat_axis=2,
-        tiled=True,
-    )[0]
-    grad_full = lax.all_gather(grad_split, "col", axis=2, tiled=True)
-    grad_left = jnp.einsum(
-        "cij,cjk->cik", grad_full, right_side, preferred_element_type=jnp.float32
-    )
-    grad_right = jnp.einsum(
-        "cij,cik->cjk", grad_full, left_side, preferred_element_type=jnp.float32
-    )
-    grad_pieces = jnp.stack([grad_left, grad_right]).astype(jnp.bfloat16)
-    grad_back = lax.all_to_all(grad_pieces, "row", split_axis=2, concat_axis=1, tiled=True)
+    if whole_cols:
+        grad_back = triangle_back(
+            grad_product.reshape(groups, share_count * row_count, col_count), own_sides
+        )
+    else:
+        grad_split = lax.all_to_all(
+            grad_product.reshape(groups, share_count, row_count, col_count),
+            "row",
+            split_axis=0,
+            concat_axis=2,
+            tiled=True,
+        )[0]
+        grad_full = lax.all_gather(grad_split, "col", axis=2, tiled=True)
+        grad_left = jnp.einsum(
+            "cij,cjk->cik", grad_full, right_side, preferred_element_type=jnp.float32
+        )
+        grad_right = jnp.einsum(
+            "cij,cik->cjk", grad_full, left_side, preferred_element_type=jnp.float32
+        )
+        grad_pieces = jnp.stack([grad_left, grad_right]).astype(jnp.bfloat16)
+        grad_back = lax.all_to_all(grad_pieces, "row", split_axis=2, concat_axis=1, tiled=True)
     grad_sides = (
         grad_back.reshape(2 * channels, row_count, col_count).astype(jnp.float32) * pair_mask[None]
     )

time: 192 us -> 182 us (0.948)
  the two profiles are of different devices: /device:TPU:16 before, /device:TPU:0 now
where the time goes in v2:
time: 182 us
  Pallas kernels  91.6 us (50%)
  starting transfers between devices  34.3 us (19%)
  waiting for transfers between devices  20.6 us (11%)
  matrix products  14.2 us (8%)
  local copies, waits for them, and re-layouts  11.9 us (7%)
  other arithmetic  7.52 us (4%)
    pallas_call x1, Pallas kernels, triangle_product(): pl.pallas_call(functools.partial(product_kernel, groups, share, rows, col...  45 us
    pallas_call x1, Pallas kernels, triangle_back(): pl.pallas_call(functools.partial(back_kernel, groups, share, rows, cols),...  36.2 us
    all_to_all x1, starting transfers between devices, summed(): lax.all_to_all(parts, 'row', split_axis=0, concat_axis=0, tiled=True)  18.7 us
    all_to_all x1, waiting for transfers between devices, summed(): lax.all_to_all(parts, 'row', split_axis=0, concat_axis=0, tiled=True)  11.9 us
    ppermute x4, starting transfers between devices, extended(): lax.ppermute(lax.slice_in_dim(block, block.shape[dim] - width, None, axis...  8.99 us
    all_to_all x1, waiting for transfers between devices, summed(): lax.all_to_all(spread, 'row', split_axis=0, concat_axis=0, tiled=True)  8.16 us
    pallas_call x1, Pallas kernels, conv_input_grad(): pl.pallas_call(functools.partial(conv_kernel, rows, cols), out_shape=jax....  7.98 us
    unnamed x73, local copies, waits for them, and re-layouts  5.55 us
  transfers between devices with their start and end apart: 10, of which 3 were waited for; matrix products, arithmetic and copies ran while one was open for 4% of the time, Pallas kernels for 6%

profile of v2, /device:TPU:0, one launch (start us, length us, event | category | flops | bytes accessed | tf_op | source)
XLA Modules:
  0.0 181.5 jit_solution(17020478407619794075)
XLA Ops:
  0.7 1.3 convert_reduce_fusion
  2.1 1.7 fusion.28
  4.4 1.6 fusion.56
  6.1 2.4 %fusion.1 = (bf16[256,8,256]{2,0,1:T(8,128)(2,1)S(1)}, f32[8,256,256]{1,2,0:T(8,128)}) fusion(f32[8,256,256]{1,2,0:T(8,128)S(1)} %fusion.56, f32[8,256]{1,0:T(8,128)S(1)} %fusion.20, bf16[128,256,1]{0,1,2:T(8,128)(2,1)S(1)} %bitcast.217, bf16[8,256,128]{2,1,0:T(8,128)(2,1)S(1)} %copy-done.2, f32[128]{0:T(128)S(1)} %copy-done.16, f32[128]{0:T(128)S(1)} %copy-done.14, ...), kind=kOutput, calls=%fused_computation.6 | convolution fusion | flops 138936320 | bytes 5858304 | tf_op jit(solution)/shard_map/rkc,ce->erk/dot_general | solution.py:371
  9.0 45.0 %triangle_product.1 = (bf16[32,32,256]{2,1,0:T(8,128)(2,1)S(1)}, bf16[4,2,256,256]{3,2,1,0:T(8,128)(2,1)S(1)}) custom-call(bf16[32,4,16,256]{3,2,1,0:T(8,128)(2,1)S(1)} %bitcast.208), custom_call_target="tpu_custom_call" | custom-call | tf_op jit(solution)/shard_map/triangle_product/pallas_call | solution.py:150
  54.8 0.7 fusion.9
  57.0 1.5 fusion.65
  58.5 3.0 %fusion.19 = f32[8,256,128]{2,1,0:T(8,128)} fusion(f32[8,256,128]{2,1,0:T(8,128)} %copy-done.8, bf16[8,256,128]{2,1,0:T(8,128)(2,1)S(1)} %copy-done.6, f32[128,8,256]{2,1,0:T(8,128)S(1)} %convert.2, f32[128]{0:T(128)S(1)} %copy-done.17, f32[128]{0:T(128)S(1)} %copy-done.15, f32[8,256]{1,0:T(8,128)S(1)} %add_rsqrt_fusion, ...), kind=kOutput, calls=%fused_computation.35 | convolution fusion | flops 137101312 | bytes 3752960 | tf_op jit(solution)/shard_map/rkd,cd->rkc/dot_general | solution.py:444
  61.5 1.7 multiply_convert_fusion
  63.5 36.2 %triangle_back.1 = bf16[32,4,16,256]{3,2,1,0:T(8,128)(2,1)S(1)} custom-call(bf16[32,32,256]{2,1,0:T(8,128)(2,1)S(1)} %bitcast.211, bf16[4,2,256,256]{3,2,1,0:T(8,128)(2,1)S(1)} %get-tuple-element.5.sides_ref), custom_call_target="tpu_custom_call" | custom-call | tf_op jit(solution)/shard_map/triangle_back/pallas_call | solution.py:176
  99.9 1.4 copy-done.5
  101.4 1.0 fusion.31
  103.2 2.3 %fusion.64 = (f32[8,256]{1,0:T(8,128)S(1)}, f32[8,256]{1,0:T(8,128)S(1)}, f32[8,256,128]{2,1,0:T(8,128)S(1)}) fusion(f32[8,256]{1,0:T(8,128)S(1)} %add_rsqrt_fusion.1, f32[8,256]{1,0:T(8,128)S(1)} %broadcast_multiply_fusion.6, bf16[8,256,128]{2,1,0:T(8,128)(2,1)S(1)} %copy-done.2, f32[128]{0:T(128)S(1)} %copy-done.14, f32[8,256,128]{2,1,0:T(8,128)S(1)} %copy-done.7, ...), kind=kOutput, calls=%fused_computation.174 | convolution fusion | flops 139718656 | bytes 10068480 | tf_op jit(solution)/shard_map/erk,ce->rkc/dot_general | solution.py:441
  105.5 1.3 fusion.30
  106.8 0.8 fusion.68
  107.6 1.3 collective-permute-start.1
  108.9 3.3 %collective-permute-start = (bf16[4,256,128]{2,1,0:T(8,128)(2,1)}, bf16[4,256,128]{2,1,0:T(8,128)(2,1)S(1)}, u32[]{:S(2)}, u32[]{:S(2)}) collective-permute-start(bf16[4,256,128]{2,1,0:T(8,128)(2,1)} %get-tuple-element.16), channel_id=1, source_target_pairs={{0,1},{1,2},{2,3},{3,4},{4,5},{5,6},{6,7},{7,8},{8,9},{9,10},{10,1... | collective-permute-start | bytes 786440 | tf_op jit(solution)/shard_map/ppermute | solution.py:21
  112.2 0.8 fusion.67
  113.1 4.4 %collective-permute-start.4 = (bf16[4,256,128]{2,1,0:T(8,128)(2,1)}, bf16[4,256,128]{2,1,0:T(8,128)(2,1)}, u32[]{:S(2)}, u32[]{:S(2)}) collective-permute-start(bf16[4,256,128]{2,1,0:T(8,128)(2,1)} %get-tuple-element.15), channel_id=1, source_target_pairs={{0,1},{1,2},{2,3},{3,4},{4,5},{5,6},{6,7},{7,8},{8,9},{9,10},{10,1... | collective-permute-start | bytes 786440 | tf_op jit(solution)/shard_map/ppermute | solution.py:21
  117.4 1.5 collective-permute-start.5
  119.7 1.0 constant_dynamic-update-slice_fusion.35
  121.2 1.0 constant_dynamic-update-slice_fusion.33
  123.9 2.4 %shifted_taps.1 = bf16[2048,1152]{1,0:T(8,128)(2,1)S(1)} custom-call(bf16[16,264,128]{2,1,0:T(8,128)(2,1)S(1)} %pad_maximum_fusion.1.ext_ref, s32[1,128]{1,0:T(1,128)S(1)} %bitcast.212), custom_call_target="tpu_custom_call" | custom-call | flops 10485760 | bytes 6291456 | tf_op jit(solution)/shard_map/shifted_taps/pallas_call | solution.py:304
  126.3 1.4 convolution_convert_fusion
  127.7 0.8 reshape.121
  128.5 18.7 %all-to-all-start = ((bf16[32,36,128]{2,1,0:T(8,128)(2,1)}), bf16[32,36,128]{2,1,0:T(8,128)(2,1)S(1)}, u32[]{:S(2)}, u32[]{:S(2)}) async-start(bf16[32,36,128]{2,1,0:T(8,128)(2,1)} %reshape.121), calls=%async_computation | async-start | bytes 655360 | tf_op jit(solution)/shard_map/all_to_all | solution.py:322
  147.2 11.9 %all-to-all-done = bf16[32,36,128]{2,1,0:T(8,128)(2,1)S(1)} async-done(((bf16[32,36,128]{2,1,0:T(8,128)(2,1)}), bf16[32,36,128]{2,1,0:T(8,128)(2,1)S(1)}, u32[]{:S(2)}, u32[]{:S(2)}) %all-to-all-start) | async-done | bytes 294944 | tf_op jit(solution)/shard_map/all_to_all | solution.py:322
  159.2 0.9 broadcast_in_dim.53
  160.1 2.6 %all-to-all-start.1 = ((f32[32,36,128]{2,1,0:T(8,128)}), f32[32,36,128]{2,1,0:T(8,128)S(1)}, u32[]{:S(2)}, u32[]{:S(2)}) async-start(f32[32,36,128]{2,1,0:T(8,128)} %broadcast_in_dim.53), calls=%async_computation.1 | async-start | bytes 1310720 | tf_op jit(solution)/shard_map/all_to_all | solution.py:327
  164.5 8.0 %conv_input_grad.1 = bf16[8,256,128]{2,1,0:T(8,128)(2,1)} custom-call(bf16[16,264,128]{2,1,0:T(8,128)(2,1)S(1)} %pad_maximum_fusion.ext_ref, bf16[4224,128]{1,0:T(8,128)(2,1)S(1)} %constant_dynamic-update-slice_fusion.weight_ref), custom_call_target="tpu_custom_call" | custom-call | flops 2214592512 | bytes 3145728 | tf_op jit(solution)/shard_map/conv_input_grad/pallas_call | solution.py:251
  172.5 8.2 %all-to-all-done.1 = f32[32,36,128]{2,1,0:T(8,128)S(1)} async-done(((f32[32,36,128]{2,1,0:T(8,128)}), f32[32,36,128]{2,1,0:T(8,128)S(1)}, u32[]{:S(2)}, u32[]{:S(2)}) %all-to-all-start.1) | async-done | bytes 589856 | tf_op jit(solution)/shard_map/all_to_all | solution.py:327
  180.7 0.9 div.80
  (112 shorter events, 9.4 us)
Async XLA Ops:
  0.6 55.9 %copy-start = (bf16[128,128]{1,0:T(8,128)(2,1)S(1)}, bf16[128,128]{1,0:T(8,128)(2,1)}, u32[]{:S(2)}) copy-start(bf16[128,128]{1,0:T(8,128)(2,1)} %param.25) | copy-start | bytes 98308
  0.6 3.8 %copy-start.2 = (bf16[8,256,128]{2,1,0:T(8,128)(2,1)S(1)}, bf16[8,256,128]{2,1,0:T(8,128)(2,1)}, u32[]{:S(2)}) copy-start(bf16[8,256,128]{2,1,0:T(8,128)(2,1)} %param.15) | copy-start | bytes 1572868
  0.7 3.1 %copy-start.11 = (bf16[128,256]{1,0:T(8,128)(2,1)S(1)}, bf16[128,256]{1,0:T(8,128)(2,1)}, u32[]{:S(2)}) copy-start(bf16[128,256]{1,0:T(8,128)(2,1)} %param.21) | copy-start | bytes 196612
  0.7 3.3 %copy-start.12 = (bf16[128,256]{1,0:T(8,128)(2,1)S(1)}, bf16[128,256]{1,0:T(8,128)(2,1)}, u32[]{:S(2)}) copy-start(bf16[128,256]{1,0:T(8,128)(2,1)} %param.22) | copy-start | bytes 196612
  0.7 3.4 %copy-start.18 = (s32[2,2]{1,0:T(2,128)S(1)}, s32[2,2]{1,0:T(2,128)}, u32[]{:S(2)}) copy-start(s32[2,2]{1,0:T(2,128)} %param.17) | copy-start | bytes 52
  0.7 3.7 %copy-start.14 = (f32[128]{0:T(128)S(1)}, f32[128]{0:T(128)}, u32[]{:S(2)}) copy-start(f32[128]{0:T(128)} %param.19) | copy-start | bytes 1540
  0.7 3.7 %copy-start.16 = (f32[128]{0:T(128)S(1)}, f32[128]{0:T(128)}, u32[]{:S(2)}) copy-start(f32[128]{0:T(128)} %param.20) | copy-start | bytes 1540
  6.1 2.4 %copy-start.3 = (f32[8,256,256]{1,2,0:T(8,128)}, f32[8,256,256]{1,2,0:T(8,128)S(1)}, u32[]{:S(2)}) copy-start(f32[8,256,256]{1,2,0:T(8,128)S(1)} %fusion.56) | copy-start | bytes 6291460
  54.0 0.8 copy-start.13
  55.6 1.0 copy-start.8
  55.6 1.4 copy-start.6
  55.6 1.4 copy-start.15
  57.0 1.5 copy-start.17
  99.8 1.6 copy-start.5
  101.4 1.6 copy-start.4
  101.4 1.9 %copy-start.7 = (f32[8,256,128]{2,1,0:T(8,128)S(1)}, f32[8,256,128]{2,1,0:T(8,128)}, u32[]{:S(2)}) copy-start(f32[8,256,128]{2,1,0:T(8,128)} %fusion.19) | copy-start | bytes 3145732
  106.8 5.4 %copy-start.9 = (bf16[8,256,128]{2,1,0:T(8,128)(2,1)S(1)}, bf16[8,256,128]{2,1,0:T(8,128)(2,1)}, u32[]{:S(2)}) copy-start(bf16[8,256,128]{2,1,0:T(8,128)(2,1)} %param.14) | copy-start | bytes 1572868
  106.8 12.1 %copy-start.1 = (s32[128]{0:T(128)S(1)}, s32[128]{0:T(128)}, u32[]{:S(2)}) copy-start(s32[128]{0:T(128)} %param.18) | copy-start | bytes 1540
  106.8 12.1 %copy-start.10 = (bf16[9,128,128]{2,1,0:T(8,128)(2,1)S(1)}, bf16[9,128,128]{2,1,0:T(8,128)(2,1)}, u32[]{:S(2)}) copy-start(bf16[9,128,128]{2,1,0:T(8,128)(2,1)} %param.27) | copy-start | bytes 884740
  107.6 55.1 %collective-permute-start.1 = (bf16[4,256,128]{2,1,0:T(8,128)(2,1)}, bf16[4,256,128]{2,1,0:T(8,128)(2,1)S(1)}, u32[]{:S(2)}, u32[]{:S(2)}) collective-permute-start(bf16[4,256,128]{2,1,0:T(8,128)(2,1)} %get-tuple-element.17), channel_id=1, source_target_pairs={{1,0},{2,1},{3,2},{4,3},{5,4},{6,5},{7,6},{8,7},{9,8},{10,9},{11,1... | collective-permute-start | bytes 786440 | tf_op jit(solution)/shard_map/ppermute | solution.py:24
  108.9 53.9 %collective-permute-start = (bf16[4,256,128]{2,1,0:T(8,128)(2,1)}, bf16[4,256,128]{2,1,0:T(8,128)(2,1)S(1)}, u32[]{:S(2)}, u32[]{:S(2)}) collective-permute-start(bf16[4,256,128]{2,1,0:T(8,128)(2,1)} %get-tuple-element.16), channel_id=1, source_target_pairs={{0,1},{1,2},{2,3},{3,4},{4,5},{5,6},{6,7},{7,8},{8,9},{9,10},{10,1... | collective-permute-start | bytes 786440 | tf_op jit(solution)/shard_map/ppermute | solution.py:21
  113.1 6.6 %collective-permute-start.4 = (bf16[4,256,128]{2,1,0:T(8,128)(2,1)}, bf16[4,256,128]{2,1,0:T(8,128)(2,1)}, u32[]{:S(2)}, u32[]{:S(2)}) collective-permute-start(bf16[4,256,128]{2,1,0:T(8,128)(2,1)} %get-tuple-element.15), channel_id=1, source_target_pairs={{0,1},{1,2},{2,3},{3,4},{4,5},{5,6},{6,7},{7,8},{8,9},{9,10},{10,1... | collective-permute-start | bytes 786440 | tf_op jit(solution)/shard_map/ppermute | solution.py:21
  117.4 3.8 %collective-permute-start.5 = (bf16[4,256,128]{2,1,0:T(8,128)(2,1)}, bf16[4,256,128]{2,1,0:T(8,128)(2,1)}, u32[]{:S(2)}, u32[]{:S(2)}) collective-permute-start(bf16[4,256,128]{2,1,0:T(8,128)(2,1)} %get-tuple-element.14), channel_id=1, source_target_pairs={{1,0},{2,1},{3,2},{4,3},{5,4},{6,5},{7,6},{8,7},{9,8},{10,9},{11,1... | collective-permute-start | bytes 786440 | tf_op jit(solution)/shard_map/ppermute | solution.py:24
  122.2 1.3 collective-permute-start.7
  122.9 0.7 collective-permute-start.6
  128.5 30.7 %all-to-all-start = ((bf16[32,36,128]{2,1,0:T(8,128)(2,1)}), bf16[32,36,128]{2,1,0:T(8,128)(2,1)S(1)}, u32[]{:S(2)}, u32[]{:S(2)}) async-start(bf16[32,36,128]{2,1,0:T(8,128)(2,1)} %reshape.121), calls=%async_computation | async-start | bytes 655360 | tf_op jit(solution)/shard_map/all_to_all | solution.py:322
  160.1 20.5 %all-to-all-start.1 = ((f32[32,36,128]{2,1,0:T(8,128)}), f32[32,36,128]{2,1,0:T(8,128)S(1)}, u32[]{:S(2)}, u32[]{:S(2)}) async-start(f32[32,36,128]{2,1,0:T(8,128)} %broadcast_in_dim.53), calls=%async_computation.1 | async-start | bytes 1310720 | tf_op jit(solution)/shard_map/all_to_all | solution.py:327
  162.8 1.3 collective-permute-start.3
  163.5 0.7 collective-permute-start.2

commit v3 on v2

--- a/solution.py
+++ b/solution.py
@@ -98,9 +98,17 @@
     lax.fori_loop(1, groups, one, 0)
 
 
-def product_kernel(groups, share, rows, cols, source_ref, product_ref, sides_ref, landed, staged, *sems):
+def product_kernel(
+    groups, share, rows, cols, source_ref, input_ref, dilation_ref, product_ref, sides_ref, taps_ref,
+    landed, staged, edge, wide, picked, *sems
+):
     me = greet(groups)
+    send_edges(groups, me, input_ref, edge, sems[4], sems[5])
     send_all(groups, me, source_ref, landed, sems[0], sems[1])
+    fill_own(rows, cols, input_ref, wide)
+    wait_edges(groups, me, input_ref, edge, sems[4], sems[5])
+    fill_edges(rows, cols, edge, wide)
+    pick_taps(rows, cols, dilation_ref[...], wide, picked, taps_ref)
     wait_all(groups, me, source_ref, landed, sems[0], sems[1])
     total = groups * rows
     for pair in range(share // 2):
@@ -143,28 +151,36 @@
     wait_all(groups, me, staged, grads_ref, sems[2], sems[3])
 
 
-def triangle_product(source):
+def triangle_product(source, conv_input, dilation):
     groups, share, two_rows, cols = source.shape
     rows = two_rows // 2
+    channels = conv_input.shape[2]
+    limit = DILATION_LIMIT
+    tall = rows + 2 * limit
     vmem = pl.BlockSpec(memory_space=pltpu.VMEM)
     return pl.pallas_call(
         functools.partial(product_kernel, groups, share, rows, cols),
         out_shape=(
             jax.ShapeDtypeStruct((groups, share * rows, cols), jnp.bfloat16),
             jax.ShapeDtypeStruct((share, 2, groups * rows, cols), jnp.bfloat16),
+            jax.ShapeDtypeStruct((rows * cols, 9 * channels), jnp.bfloat16),
         ),
-        in_specs=[vmem],
-        out_specs=(vmem, vmem),
+        in_specs=[vmem] * 3,
+        out_specs=(vmem, vmem, vmem),
         scratch_shapes=[
             pltpu.VMEM(source.shape, jnp.bfloat16),
             pltpu.VMEM((groups, share * rows, cols), jnp.bfloat16),
+            pltpu.VMEM((2, limit, cols, channels), jnp.bfloat16),
+            pltpu.VMEM((tall, cols + 2 * limit, channels), jnp.float32),
+            pltpu.VMEM((3, tall, cols, channels), jnp.float32),
         ]
-        + [pltpu.SemaphoreType.DMA((groups,))] * 4,
+        + [pltpu.SemaphoreType.DMA((groups,))] * 4
+        + [pltpu.SemaphoreType.DMA((2,))] * 2,
         compiler_params=pltpu.CompilerParams(
-            vmem_limit_bytes=32 * 2**20, collective_id=0, has_side_effects=True
+            vmem_limit_bytes=40 * 2**20, collective_id=0, has_side_effects=True
         ),
         name="triangle_product",
-    )(source)
+    )(source, conv_input, dilation[None, :])
 
 
 def triangle_back(source, sides):
@@ -192,27 +208,77 @@
     return jnp.swapaxes(weight.reshape(depth, 2, wide // 2), 1, 2).reshape(depth, wide)
 
 
-def tap_weights(conv_weight, dilation):
-    by_tap = jnp.swapaxes(conv_weight, 1, 2)
-    blocks = []
-    for amount in range(1, DILATION_LIMIT + 1):
-        chosen = jnp.where(dilation == amount, by_tap, jnp.zeros((), by_tap.dtype))
-        for up in range(3):
-            blocks += [chosen[3 * up], chosen[3 * up + 2]]
-        blocks += [chosen[1], chosen[7]]
-    return jnp.concatenate(blocks + [by_tap[4]], axis=0)
-
-
-def conv_kernel(rows, cols, ext_ref, weight_ref, out_ref, wide_ref, sides_ref):
-    limit = DILATION_LIMIT
-    wide_ref[...] = ext_ref[...].astype(jnp.float32)
-    channels = ext_ref.shape[2]
-    for amount in range(1, limit + 1):
-        for side, sign in ((0, 1), (1, -1)):
-            sides_ref[amount - 1, :, :, side * channels : (side + 1) * channels] = wide_ref[
-                :, limit + sign * amount : limit + sign * amount + cols, :
-            ].astype(jnp.bfloat16)
-    sides_ref[limit, :, :, :channels] = wide_ref[:, limit : limit + cols, :].astype(jnp.bfloat16)
+def edge_copies(groups, me, block_ref, edge_ref, send_sem, recv_sem):
+    rows = block_ref.shape[0]
+    limit = DILATION_LIMIT
+
+    def copy(source, slot, peer):
+        return pltpu.make_async_remote_copy(
+            src_ref=source,
+            dst_ref=edge_ref.at[slot],
+            send_sem=send_sem.at[slot],
+            recv_sem=recv_sem.at[slot],
+            device_id={"row": peer},
+            device_id_type=pl.DeviceIdType.MESH,
+        )
+
+    before = copy(block_ref.at[pl.ds(0, limit)], 1, lax.rem(me + groups - 1, groups))
+    after = copy(block_ref.at[pl.ds(rows - limit, limit)], 0, lax.rem(me + 1, groups))
+    return before, after
+
+
+def send_edges(groups, me, block_ref, edge_ref, send_sem, recv_sem):
+    before, after = edge_copies(groups, me, block_ref, edge_ref, send_sem, recv_sem)
+
+    @pl.when(me > 0)
+    def _():
+        before.start()
+
+    @pl.when(me < groups - 1)
+    def _():
+        after.start()
+
+    @pl.when(me == 0)
+    def _():
+        edge_ref[0] = jnp.zeros(edge_ref.shape[1:], edge_ref.dtype)
+
+    @pl.when(me == groups - 1)
+    def _():
+        edge_ref[1] = jnp.zeros(edge_ref.shape[1:], edge_ref.dtype)
+
+
+def wait_edges(groups, me, block_ref, edge_ref, send_sem, recv_sem):
+    before, after = edge_copies(groups, me, block_ref, edge_ref, send_sem, recv_sem)
+
+    @pl.when(me > 0)
+    def _():
+        before.wait_send()
+        after.wait_recv()
+
+    @pl.when(me < groups - 1)
+    def _():
+        after.wait_send()
+        before.wait_recv()
+
+
+def fill_own(rows, cols, block_ref, wide_ref):
+    limit = DILATION_LIMIT
+    tall, _, channels = wide_ref.shape
+    margin = jnp.zeros((tall, limit, channels), jnp.float32)
+    wide_ref[:, :limit, :] = margin
+    wide_ref[:, limit + cols :, :] = margin
+    wide_ref[limit : limit + rows, limit : limit + cols, :] = block_ref[...].astype(jnp.float32)
+
+
+def fill_edges(rows, cols, edge_ref, wide_ref):
+    limit = DILATION_LIMIT
+    wide_ref[:limit, limit : limit + cols, :] = edge_ref[0].astype(jnp.float32)
+    wide_ref[limit + rows :, limit : limit + cols, :] = edge_ref[1].astype(jnp.float32)
+
+
+def conv_rows(cols, first, last, weight_ref, out_ref, sides_ref):
+    limit = DILATION_LIMIT
+    channels = out_ref.shape[2]
 
     def one_row(row, carry):
         base = row + limit
@@ -242,7 +308,129 @@
         out_ref[row] = total.astype(out_ref.dtype)
         return carry
 
-    lax.fori_loop(0, rows, one_row, 0)
+    lax.fori_loop(first, last, one_row, 0)
+
+
+def split_columns(cols, first, last, wide_ref, sides_ref):
+    limit = DILATION_LIMIT
+    channels = wide_ref.shape[2]
+    for amount in range(1, limit + 1):
+        for side, sign in ((0, 1), (1, -1)):
+            sides_ref[amount - 1, first:last, :, side * channels : (side + 1) * channels] = wide_ref[
+                first:last, limit + sign * amount : limit + sign * amount + cols, :
+            ].astype(jnp.bfloat16)
+    sides_ref[limit, first:last, :, :channels] = wide_ref[first:last, limit : limit + cols, :].astype(
+        jnp.bfloat16
+    )
+
+
+def last_kernel(
+    groups, rows, cols, grad_ref, terms_ref, weight_ref, out_ref, sum_ref, edge, wide, sides, landed, own, *sems
+):
+    limit = DILATION_LIMIT
+    me = greet(groups)
+    send_edges(groups, me, grad_ref, edge, sems[0], sems[1])
+    send_all(groups, me, terms_ref, landed, sems[2], sems[3])
+    fill_own(rows, cols, grad_ref, wide)
+    split_columns(cols, limit, limit + rows, wide, sides)
+    wait_edges(groups, me, grad_ref, edge, sems[0], sems[1])
+    fill_edges(rows, cols, edge, wide)
+    split_columns(cols, 0, limit, wide, sides)
+    split_columns(cols, limit + rows, rows + 2 * limit, wide, sides)
+    wait_all(groups, me, terms_ref, landed, sems[2], sems[3])
+
+    def add(index, total):
+        return total + landed[index].astype(jnp.float32)
+
+    total = lax.fori_loop(0, groups, add, jnp.zeros(landed.shape[1:], jnp.float32))
+    own[...] = total.astype(jnp.bfloat16)
+
+    def spread(peer):
+        return pltpu.make_async_remote_copy(
+            src_ref=own,
+            dst_ref=sum_ref.at[me],
+            send_sem=sems[4].at[peer],
+            recv_sem=sems[5].at[me],
+            device_id={"row": peer},
+            device_id_type=pl.DeviceIdType.MESH,
+        )
+
+    def one(step, carry):
+        spread(lax.rem(me + step, groups)).start()
+        return carry
+
+    lax.fori_loop(1, groups, one, 0)
+    sum_ref[me] = own[...]
+    conv_rows(cols, 0, rows, weight_ref, out_ref, sides)
+
+    def finish(step, carry):
+        peer = lax.rem(me + groups - step, groups)
+        pltpu.make_async_remote_copy(
+            src_ref=own,
+            dst_ref=sum_ref.at[peer],
+            send_sem=sems[4].at[peer],
+            recv_sem=sems[5].at[peer],
+            device_id={"row": peer},
+            device_id_type=pl.DeviceIdType.MESH,
+        ).wait()
+        return carry
+
+    lax.fori_loop(1, groups, finish, 0)
+
+
+def conv_and_sum(gradient, terms, weights):
+    rows, cols, channels = gradient.shape
+    groups = terms.shape[0]
+    limit = DILATION_LIMIT
+    tall = rows + 2 * limit
+    vmem = pl.BlockSpec(memory_space=pltpu.VMEM)
+    return pl.pallas_call(
+        functools.partial(last_kernel, groups, rows, cols),
+        out_shape=(
+            jax.ShapeDtypeStruct(gradient.shape, jnp.bfloat16),
+            jax.ShapeDtypeStruct(terms.shape, jnp.bfloat16),
+        ),
+        in_specs=[vmem] * 3,
+        out_specs=(vmem, vmem),
+        scratch_shapes=[
+            pltpu.VMEM((2, limit, cols, channels), jnp.bfloat16),
+            pltpu.VMEM((tall, cols + 2 * limit, channels), jnp.float32),
+            pltpu.VMEM((limit + 1, tall, cols, 2 * channels), jnp.bfloat16),
+            pltpu.VMEM(terms.shape, jnp.bfloat16),
+            pltpu.VMEM(terms.shape[1:], jnp.bfloat16),
+        ]
+        + [pltpu.SemaphoreType.DMA((2,))] * 2
+        + [pltpu.SemaphoreType.DMA((groups,))] * 4,
+        compiler_params=pltpu.CompilerParams(
+            vmem_limit_bytes=40 * 2**20, collective_id=2, has_side_effects=True
+        ),
+        name="conv_and_sum",
+    )(gradient, terms, weights)
+
+
+def tap_weights(conv_weight, dilation):
+    by_tap = jnp.swapaxes(conv_weight, 1, 2)
+    blocks = []
+    for amount in range(1, DILATION_LIMIT + 1):
+        chosen = jnp.where(dilation == amount, by_tap, jnp.zeros((), by_tap.dtype))
+        for up in range(3):
+            blocks += [chosen[3 * up], chosen[3 * up + 2]]
+        blocks += [chosen[1], chosen[7]]
+    return jnp.concatenate(blocks + [by_tap[4]], axis=0)
+
+
+def conv_kernel(rows, cols, ext_ref, weight_ref, out_ref, wide_ref, sides_ref):
+    limit = DILATION_LIMIT
+    wide_ref[...] = ext_ref[...].astype(jnp.float32)
+    channels = ext_ref.shape[2]
+    for amount in range(1, limit + 1):
+        for side, sign in ((0, 1), (1, -1)):
+            sides_ref[amount - 1, :, :, side * channels : (side + 1) * channels] = wide_ref[
+                :, limit + sign * amount : limit + sign * amount + cols, :
+            ].astype(jnp.bfloat16)
+    sides_ref[limit, :, :, :channels] = wide_ref[:, limit : limit + cols, :].astype(jnp.bfloat16)
+
+    conv_rows(cols, 0, rows, weight_ref, out_ref, sides_ref)
 
 
 def conv_input_grad(bordered, weights, rows, cols):
@@ -265,11 +453,9 @@
     )(bordered, weights)
 
 
-def shift_kernel(rows, cols, ext_ref, dilation_ref, out_ref, wide_ref, picked_ref):
-    limit = DILATION_LIMIT
-    channels = ext_ref.shape[2]
-    wide_ref[...] = ext_ref[...].astype(jnp.float32)
-    dilation = dilation_ref[...]
+def pick_taps(rows, cols, dilation, wide_ref, picked_ref, out_ref):
+    limit = DILATION_LIMIT
+    channels = wide_ref.shape[2]
 
     def columns(row, carry):
         for side in range(3):
@@ -297,6 +483,11 @@
         return carry
 
     lax.fori_loop(0, rows, one_row, 0)
+
+
+def shift_kernel(rows, cols, ext_ref, dilation_ref, out_ref, wide_ref, picked_ref):
+    wide_ref[...] = ext_ref[...].astype(jnp.float32)
+    pick_taps(rows, cols, dilation_ref[...], wide_ref, picked_ref, out_ref)
 
 
 def shifted_taps(bordered, dilation, rows, cols):
@@ -372,8 +563,8 @@
     gate_sig = jax.nn.sigmoid(gate_lin)
     both_sides = (projected * gate_sig * pair_mask[None]).astype(jnp.bfloat16)
     if whole_cols:
-        product, own_sides = triangle_product(
-            both_sides.reshape(groups, share_count, 2 * row_count, col_count)
+        product, own_sides, shifted_input = triangle_product(
+            both_sides.reshape(groups, share_count, 2 * row_count, col_count), convolution_input, dilation
         )
         product = product.reshape(channels, row_count, col_count)
     else:
@@ -447,17 +638,26 @@
     pair_gradient = (cotangent + norm_back(grad_in, in_hat, in_inv, in_gain, 2)).astype(
         jnp.bfloat16
     )
-    bordered_input = extended(convolution_input, (("row", 0), ("col", 1)), DILATION_LIMIT)
-    bordered_gradient = extended(pair_gradient, (("row", 0), ("col", 1)), DILATION_LIMIT)
-    input_grad = conv_input_grad(bordered_gradient, tap_weights(conv_weight, dilation), row_count, col_count)
-    shifted_input = shifted_taps(bordered_input, dilation, row_count, col_count)
+    weights = tap_weights(conv_weight, dilation)
+    if not whole_cols:
+        bordered_input = extended(convolution_input, (("row", 0), ("col", 1)), DILATION_LIMIT)
+        shifted_input = shifted_taps(bordered_input, dilation, row_count, col_count)
     weight_terms = lax.dot_general(
         shifted_input,
         pair_gradient.reshape(row_count * col_count, channels),
         (((0,), (0,)), ((), ())),
         preferred_element_type=jnp.float32,
     )
-    weight_total = summed(weight_terms, groups)
+    if whole_cols:
+        part = weight_terms.shape[0] // groups
+        terms = weight_terms.astype(jnp.bfloat16).reshape(groups, part, channels)
+        terms = jnp.pad(terms, ((0, 0), (0, -part % 16), (0, 0)))
+        input_grad, weight_total = conv_and_sum(pair_gradient, terms, weights)
+        weight_total = weight_total[:, :part].astype(jnp.float32)
+    else:
+        bordered_gradient = extended(pair_gradient, (("row", 0), ("col", 1)), DILATION_LIMIT)
+        input_grad = conv_input_grad(bordered_gradient, weights, row_count, col_count)
+        weight_total = summed(weight_terms, groups)
     return (input_grad, weight_total.reshape(9, channels, channels) / total_rows)
 
 

time: 182 us -> 151 us (0.83); the launches traced: 182 us -> 148 us
  starting transfers between devices: 34.3 us -> 0 us
  Pallas kernels: 91.6 us -> 116 us
  waiting for transfers between devices: 20.6 us -> 0 us
  local copies, waits for them, and re-layouts: 11.9 us -> 9.77 us
  other arithmetic: 7.52 us -> 5.62 us
    pallas_call x2 -> x1, Pallas kernels: 10.3 us -> 34.8 us  [conv_and_sum(): pl.pallas_call(functools.partial(last_kernel, groups, rows, cols), out_sh...]
    all_to_all x2 -> x0, starting transfers between devices: 21.3 us -> none  [the longest x1 18.7 us: summed(): lax.all_to_all(parts, 'row', split_axis=0, concat_axis=0, tiled=True)]
    all_to_all x2 -> x0, waiting for transfers between devices: 20.1 us -> none  [the longest x1 11.9 us: summed(): lax.all_to_all(parts, 'row', split_axis=0, concat_axis=0, tiled=True)]
    ppermute x8 -> x0, starting transfers between devices: 13 us -> none  [the longest x4 8.99 us: extended(): lax.ppermute(lax.slice_in_dim(block, block.shape[dim] - width, None, axis...]
    unnamed x73 -> x76, local copies, waits for them, and re-layouts: 5.55 us -> 7.64 us
  transfers between devices with their start and end apart: 10 -> 0, of which waited for: 3 -> 0; matrix products, arithmetic and copies ran while one was open for 4% -> 0% of each run, Pallas kernels for 6% -> 0%
where the time goes in v3:
time: 151 us; the launch traced here: 148 us
  Pallas kernels  116 us (77%)
  matrix products  15.8 us (10%)
  local copies, waits for them, and re-layouts  9.77 us (6%)
  other arithmetic  5.62 us (4%)
    pallas_call x1, Pallas kernels, triangle_product(): pl.pallas_call(functools.partial(product_kernel, groups, share, rows, col...  43.6 us
    pallas_call x1, Pallas kernels, triangle_back(): pl.pallas_call(functools.partial(back_kernel, groups, share, rows, cols),...  37.4 us
    pallas_call x1, Pallas kernels, conv_and_sum(): pl.pallas_call(functools.partial(last_kernel, groups, rows, cols), out_sh...  34.8 us
    unnamed x76, local copies, waits for them, and re-layouts  7.64 us
    dot_general x1, matrix products, on_device(): jnp.einsum('rkd,cd->rkc', grad_gate, out_gate_weight, preferred_element_t...  3.05 us

profile of v3, /device:TPU:0, one launch (start us, length us, event | category | flops | bytes accessed | tf_op | source)
XLA Modules:
  0.0 148.3 jit_solution(342099483488301207)
XLA Ops:
  0.7 1.3 convert_reduce_fusion
  2.0 1.7 %fusion.28 = f32[8,256]{1,0:T(8,128)S(1)} fusion(bf16[8,256,128]{2,1,0:T(8,128)(2,1)} %param.15, f32[8,256]{1,0:T(8,128)S(1)} %broadcast_multiply_fusion.5), kind=kLoop, calls=%fused_computation.43 | loop fusion | flops 1046528 | bytes 540672 | tf_op jit(solution)/shard_map/reduce_sum | solution.py:32
  3.8 1.8 %fusion.9 = f32[8,256,128]{2,1,0:T(8,128)} fusion(bf16[128,128]{1,0:T(8,128)(2,1)S(1)} %copy-done.13, bf16[8,256,128]{2,1,0:T(8,128)(2,1)S(1)} %copy-done.4, f32[128]{0:T(128)S(1)} %copy-done.16, f32[128]{0:T(128)S(1)} %copy-done.14, f32[8,256]{1,0:T(8,128)S(1)} %add_rsqrt_fusion.1, f32[8,256]{1,0:T(8,128)S(1)} %broadcast_multiply_fusion.5), kind=kOutput, calls=%fused_computation.22 | convolution fusion | flops 69468160 | bytes 1623040 | tf_op jit(solution)/shard_map/rkc,cd->rkd/dot_general | solution.py:598
  5.6 0.1 copy.27
  5.7 1.6 %fusion.56 = f32[8,256,256]{1,2,0:T(8,128)S(1)} fusion(bf16[128,256,1]{0,1,2:T(8,128)(2,1)S(1)} %bitcast.217, bf16[8,256,128]{2,1,0:T(8,128)(2,1)S(1)} %copy-done.4, f32[128]{0:T(128)S(1)} %copy-done.16, f32[128]{0:T(128)S(1)} %copy-done.14, f32[8,256]{1,0:T(8,128)S(1)} %add_rsqrt_fusion.1, f32[8,256]{1,0:T(8,128)S(1)} %broadcast_multiply_fusion.5), kind=kOutput, calls=%fused_computation.139 | convolution fusion | flops 135790592 | bytes 2704384 | tf_op jit(solution)/shard_map/rkc,ce->erk/dot_general | solution.py:559
  7.4 0.3 fusion.20
  7.7 0.1 copy.28
  7.9 0.9 copy-done.5
  8.7 2.4 %fusion.1 = (bf16[256,8,256]{2,0,1:T(8,128)(2,1)S(1)}, f32[8,256,256]{1,2,0:T(8,128)}) fusion(f32[8,256,256]{1,2,0:T(8,128)S(1)} %fusion.56, f32[8,256]{1,0:T(8,128)S(1)} %fusion.20, bf16[128,256,1]{0,1,2:T(8,128)(2,1)S(1)} %bitcast.219, bf16[8,256,128]{2,1,0:T(8,128)(2,1)S(1)} %copy-done.4, f32[128]{0:T(128)S(1)} %copy-done.16, f32[128]{0:T(128)S(1)} %copy-done.14, ...), kind=kOutput, calls=%fused_computation.6 | convolution fusion | flops 138936320 | bytes 5858304 | tf_op jit(solution)/shard_map/rkc,ce->erk/dot_general | solution.py:562
  11.2 0.6 copy.29
  11.8 0.5 copy-done.1
  12.2 43.6 %triangle_product.1 = (bf16[32,32,256]{2,1,0:T(8,128)(2,1)S(1)}, bf16[4,2,256,256]{3,2,1,0:T(8,128)(2,1)S(1)}, bf16[2048,1152]{1,0:T(8,128)(2,1)S(1)}) custom-call(bf16[32,4,16,256]{3,2,1,0:T(8,128)(2,1)S(1)} %bitcast.208, bf16[8,256,128]{2,1,0:T(8,128)(2,1)S(1)} %copy-done.1, s32[1,128]{1,0:T(1,128)S(1)} %bitcast.213), custom_call_target="tpu_custom_call" | custom-call | tf_op jit(solution)/shard_map/triangle_product/pallas_call | solution.py:161
  55.8 2.1 %copy-done.3 = bf16[2048,1152]{1,0:T(8,128)(2,1)} copy-done((bf16[2048,1152]{1,0:T(8,128)(2,1)}, bf16[2048,1152]{1,0:T(8,128)(2,1)S(1)}, u32[]{:S(2)}) %copy-start.3) | copy-done | bytes 4718616
  58.1 0.1 convert_reduce_fusion.1
  58.2 0.3 multiply_reduce_fusion.1
  58.6 0.5 copy-done.8
  59.1 3.0 %fusion.19 = f32[8,256,128]{2,1,0:T(8,128)} fusion(f32[8,256,128]{2,1,0:T(8,128)} %fusion.9, bf16[8,256,128]{2,1,0:T(8,128)(2,1)S(1)} %copy-done.8, f32[128,8,256]{2,1,0:T(8,128)S(1)} %convert.2, f32[128]{0:T(128)S(1)} %copy-done.17, f32[128]{0:T(128)S(1)} %copy-done.15, f32[8,256]{1,0:T(8,128)S(1)} %add_rsqrt_fusion, ...), kind=kOutput, calls=%fused_computation.35 | convolution fusion | flops 137101312 | bytes 3752960 | tf_op jit(solution)/shard_map/rkd,cd->rkc/dot_general | solution.py:635
  62.1 1.9 %fusion.65 = (f32[8,256]{1,0:T(8,128)S(1)}, f32[8,256]{1,0:T(8,128)S(1)}, f32[128,8,256]{2,0,1:T(8,128)S(1)}) fusion(f32[8,256]{1,0:T(8,128)S(1)} %add_rsqrt_fusion, f32[8,256]{1,0:T(8,128)S(1)} %broadcast_multiply_fusion.4, f32[128,8,256]{2,1,0:T(8,128)S(1)} %convert.2, f32[128]{0:T(128)S(1)} %copy-done.15, bf16[128,128]{1,0:T(8,128)(2,1)S(1)} %copy-done, ...), kind=kOutput, calls=%fused_computation.166 | convolution fusion | flops 69464064 | bytes 3736064 | tf_op jit(solution)/shard_map/rkd,cd->crk/dot_general | solution.py:603
  64.0 0.5 multiply_convert_fusion
  64.5 0.3 copy.31
  64.8 37.4 %triangle_back.1 = bf16[32,4,16,256]{3,2,1,0:T(8,128)(2,1)S(1)} custom-call(bf16[32,32,256]{2,1,0:T(8,128)(2,1)S(1)} %bitcast.211, bf16[4,2,256,256]{3,2,1,0:T(8,128)(2,1)S(1)} %get-tuple-element.8.sides_ref), custom_call_target="tpu_custom_call" | custom-call | tf_op jit(solution)/shard_map/triangle_back/pallas_call | solution.py:192
  102.2 0.2 convert.3
  102.4 1.4 copy-done.7
  103.8 1.1 fusion.31
  104.9 2.3 %fusion.64 = (f32[8,256]{1,0:T(8,128)S(1)}, f32[8,256]{1,0:T(8,128)S(1)}, f32[8,256,128]{2,1,0:T(8,128)S(1)}) fusion(f32[8,256]{1,0:T(8,128)S(1)} %add_rsqrt_fusion.1, f32[8,256]{1,0:T(8,128)S(1)} %broadcast_multiply_fusion.5, bf16[8,256,128]{2,1,0:T(8,128)(2,1)S(1)} %copy-done.4, f32[128]{0:T(128)S(1)} %copy-done.14, f32[8,256,128]{2,1,0:T(8,128)S(1)} %copy-done.9, ...), kind=kOutput, calls=%fused_computation.165 | convolution fusion | flops 139718656 | bytes 10068480 | tf_op jit(solution)/shard_map/erk,ce->rkc/dot_general | solution.py:632
  107.2 1.3 fusion.30.grad_ref
  108.5 1.4 convolution_convert_fusion
  110.1 0.8 copy-done.10
  110.9 0.2 copy.37
  111.7 34.8 %conv_and_sum.1 = (bf16[8,256,128]{2,1,0:T(8,128)(2,1)S(1)}, bf16[32,48,128]{2,1,0:T(8,128)(2,1)S(1)}) custom-call(bf16[8,256,128]{2,1,0:T(8,128)(2,1)S(1)} %fusion.30.grad_ref, bf16[32,48,128]{2,1,0:T(8,128)(2,1)S(1)} %pad.4.terms_ref, bf16[4224,128]{1,0:T(8,128)(2,1)S(1)} %constant_dynamic-update-slice_fusion.weight_ref), custom_call_target="tpu_custom_call" | custom-call | tf_op jit(solution)/shard_map/conv_and_sum/pallas_call | solution.py:387
  146.6 0.9 div.80
  147.5 0.8 copy.99
  (87 shorter events, 0.8 us)
Async XLA Ops:
  0.6 57.9 %copy-start = (bf16[128,128]{1,0:T(8,128)(2,1)S(1)}, bf16[128,128]{1,0:T(8,128)(2,1)}, u32[]{:S(2)}) copy-start(bf16[128,128]{1,0:T(8,128)(2,1)} %param.25) | copy-start | bytes 98308
  0.6 3.1 %copy-start.4 = (bf16[8,256,128]{2,1,0:T(8,128)(2,1)S(1)}, bf16[8,256,128]{2,1,0:T(8,128)(2,1)}, u32[]{:S(2)}) copy-start(bf16[8,256,128]{2,1,0:T(8,128)(2,1)} %param.15) | copy-start | bytes 1572868
  0.7 3.1 %copy-start.14 = (f32[128]{0:T(128)S(1)}, f32[128]{0:T(128)}, u32[]{:S(2)}) copy-start(f32[128]{0:T(128)} %param.19) | copy-start | bytes 1540
  0.7 3.1 %copy-start.13 = (bf16[128,128]{1,0:T(8,128)(2,1)S(1)}, bf16[128,128]{1,0:T(8,128)(2,1)}, u32[]{:S(2)}) copy-start(bf16[128,128]{1,0:T(8,128)(2,1)} %param.26) | copy-start | bytes 98308
  0.7 3.1 %copy-start.16 = (f32[128]{0:T(128)S(1)}, f32[128]{0:T(128)}, u32[]{:S(2)}) copy-start(f32[128]{0:T(128)} %param.20) | copy-start | bytes 1540
  3.7 1.8 %copy-start.11 = (bf16[128,256]{1,0:T(8,128)(2,1)S(1)}, bf16[128,256]{1,0:T(8,128)(2,1)}, u32[]{:S(2)}) copy-start(bf16[128,256]{1,0:T(8,128)(2,1)} %param.21) | copy-start | bytes 196612
  5.7 1.7 %copy-start.18 = (s32[2,2]{1,0:T(2,128)S(1)}, s32[2,2]{1,0:T(2,128)}, u32[]{:S(2)}) copy-start(s32[2,2]{1,0:T(2,128)} %param.17) | copy-start | bytes 52
  5.7 2.0 %copy-start.12 = (bf16[128,256]{1,0:T(8,128)(2,1)S(1)}, bf16[128,256]{1,0:T(8,128)(2,1)}, u32[]{:S(2)}) copy-start(bf16[128,256]{1,0:T(8,128)(2,1)} %param.22) | copy-start | bytes 196612
  7.4 1.4 copy-start.5
  11.2 1.0 copy-start.1
  11.2 1.0 copy-start.2
  55.8 2.1 %copy-start.3 = (bf16[2048,1152]{1,0:T(8,128)(2,1)}, bf16[2048,1152]{1,0:T(8,128)(2,1)S(1)}, u32[]{:S(2)}) copy-start(bf16[2048,1152]{1,0:T(8,128)(2,1)S(1)} %get-tuple-element.9) | copy-start | bytes 14155780
  58.0 1.0 copy-start.8
  58.0 1.0 copy-start.15
  58.0 1.0 copy-start.17
  102.2 1.6 %copy-start.7 = (f32[8,256,256]{1,2,0:T(8,128)S(1)}, f32[8,256,256]{1,2,0:T(8,128)}, u32[]{:S(2)}) copy-start(f32[8,256,256]{1,2,0:T(8,128)} %get-tuple-element.25) | copy-start | bytes 6291460
  102.2 2.7 %copy-start.6 = (f32[8,256,256]{1,2,0:T(8,128)S(1)}, f32[8,256,256]{1,2,0:T(8,128)}, u32[]{:S(2)}) copy-start(f32[8,256,256]{1,2,0:T(8,128)} %copy-done.5) | copy-start | bytes 6291460
  102.2 2.7 %copy-start.9 = (f32[8,256,128]{2,1,0:T(8,128)S(1)}, f32[8,256,128]{2,1,0:T(8,128)}, u32[]{:S(2)}) copy-start(f32[8,256,128]{2,1,0:T(8,128)} %fusion.19) | copy-start | bytes 3145732
  103.8 4.7 %slice-start = ((s8[4718592]{0:T(1024)(128)(4,1)}), s8[4194304]{0:T(1024)(128)(4,1)S(1)}, s32[]{:S(2)}) async-start(s8[4718592]{0:T(1024)(128)(4,1)} %bitcast.214), calls=%async_computation | async-start | bytes 8388608
  104.9 3.6 %slice-start.1 = ((s8[4718592]{0:T(1024)(128)(4,1)}), s8[524288]{0:T(1024)(128)(4,1)S(1)}, s32[]{:S(2)}) async-start(s8[4718592]{0:T(1024)(128)(4,1)} %bitcast.214), calls=%async_computation.1 | async-start | bytes 1048576
  110.0 1.0 copy-start.10

commit v4 on v3

--- a/solution.py
+++ b/solution.py
@@ -330,57 +330,101 @@
     limit = DILATION_LIMIT
     me = greet(groups)
     send_edges(groups, me, grad_ref, edge, sems[0], sems[1])
-    send_all(groups, me, terms_ref, landed, sems[2], sems[3])
+    count = terms_ref.shape[0]
+    place = (me * count + groups - 1) // groups
+    is_owner = (place * groups) // count == me
+
+    def term(index, slot, source):
+        return pltpu.make_async_remote_copy(
+            src_ref=terms_ref.at[index],
+            dst_ref=landed.at[source],
+            send_sem=sems[2].at[index],
+            recv_sem=sems[3].at[slot],
+            device_id={"row": (index * groups) // count},
+            device_id_type=pl.DeviceIdType.MESH,
+        )
+
+    def give(step, carry):
+        index = lax.rem(place + step, count)
+
+        @pl.when((index * groups) // count != me)
+        def _():
+            term(index, me, me).start()
+
+        return carry
+
+    lax.fori_loop(0, count, give, 0)
     fill_own(rows, cols, grad_ref, wide)
     split_columns(cols, limit, limit + rows, wide, sides)
     wait_edges(groups, me, grad_ref, edge, sems[0], sems[1])
     fill_edges(rows, cols, edge, wide)
     split_columns(cols, 0, limit, wide, sides)
     split_columns(cols, limit + rows, rows + 2 * limit, wide, sides)
-    wait_all(groups, me, terms_ref, landed, sems[2], sems[3])
-
-    def add(index, total):
-        return total + landed[index].astype(jnp.float32)
-
-    total = lax.fori_loop(0, groups, add, jnp.zeros(landed.shape[1:], jnp.float32))
-    own[...] = total.astype(jnp.bfloat16)
-
-    def spread(peer):
+
+    def given(index, carry):
+        @pl.when((index * groups) // count != me)
+        def _():
+            term(index, me, me).wait_send()
+
+        return carry
+
+    def spread(peer, slot):
         return pltpu.make_async_remote_copy(
             src_ref=own,
-            dst_ref=sum_ref.at[me],
+            dst_ref=sum_ref.at[slot],
             send_sem=sems[4].at[peer],
-            recv_sem=sems[5].at[me],
+            recv_sem=sems[5].at[slot],
             device_id={"row": peer},
             device_id_type=pl.DeviceIdType.MESH,
         )
 
-    def one(step, carry):
-        spread(lax.rem(me + step, groups)).start()
-        return carry
-
-    lax.fori_loop(1, groups, one, 0)
-    sum_ref[me] = own[...]
+    @pl.when(is_owner)
+    def _():
+        landed[me] = terms_ref[place]
+
+        def arrive(step, carry):
+            peer = lax.rem(me + groups - step, groups)
+            term(place, peer, peer).wait_recv()
+            return carry
+
+        lax.fori_loop(1, groups, arrive, 0)
+
+        def add(index, total):
+            return total + landed[index].astype(jnp.float32)
+
+        total = lax.fori_loop(0, groups, add, jnp.zeros(landed.shape[1:], jnp.float32))
+        own[...] = total.astype(jnp.bfloat16)
+
+        def one(step, carry):
+            spread(lax.rem(me + step, groups), place).start()
+            return carry
+
+        lax.fori_loop(1, groups, one, 0)
+        sum_ref[place] = own[...]
+
     conv_rows(cols, 0, rows, weight_ref, out_ref, sides)
-
-    def finish(step, carry):
-        peer = lax.rem(me + groups - step, groups)
-        pltpu.make_async_remote_copy(
-            src_ref=own,
-            dst_ref=sum_ref.at[peer],
-            send_sem=sems[4].at[peer],
-            recv_sem=sems[5].at[peer],
-            device_id={"row": peer},
-            device_id_type=pl.DeviceIdType.MESH,
-        ).wait()
-        return carry
-
-    lax.fori_loop(1, groups, finish, 0)
-
-
-def conv_and_sum(gradient, terms, weights):
+    lax.fori_loop(0, count, given, 0)
+
+    @pl.when(is_owner)
+    def _():
+        def sent(step, carry):
+            spread(lax.rem(me + step, groups), place).wait_send()
+            return carry
+
+        lax.fori_loop(1, groups, sent, 0)
+
+    def finish(index, carry):
+        @pl.when((index * groups) // count != me)
+        def _():
+            spread(me, index).wait_recv()
+
+        return carry
+
+    lax.fori_loop(0, count, finish, 0)
+
+
+def conv_and_sum(gradient, terms, weights, groups):
     rows, cols, channels = gradient.shape
-    groups = terms.shape[0]
     limit = DILATION_LIMIT
     tall = rows + 2 * limit
     vmem = pl.BlockSpec(memory_space=pltpu.VMEM)
@@ -396,7 +440,7 @@
             pltpu.VMEM((2, limit, cols, channels), jnp.bfloat16),
             pltpu.VMEM((tall, cols + 2 * limit, channels), jnp.float32),
             pltpu.VMEM((limit + 1, tall, cols, 2 * channels), jnp.bfloat16),
-            pltpu.VMEM(terms.shape, jnp.bfloat16),
+            pltpu.VMEM((groups,) + terms.shape[1:], jnp.bfloat16),
             pltpu.VMEM(terms.shape[1:], jnp.bfloat16),
         ]
         + [pltpu.SemaphoreType.DMA((2,))] * 2
@@ -649,11 +693,13 @@
         preferred_element_type=jnp.float32,
     )
     if whole_cols:
-        part = weight_terms.shape[0] // groups
-        terms = weight_terms.astype(jnp.bfloat16).reshape(groups, part, channels)
-        terms = jnp.pad(terms, ((0, 0), (0, -part % 16), (0, 0)))
-        input_grad, weight_total = conv_and_sum(pair_gradient, terms, weights)
-        weight_total = weight_total[:, :part].astype(jnp.float32)
+        deep = weight_terms.shape[0]
+        part = 16 * (-(-deep // (16 * groups)))
+        while deep % part:
+            part += 16
+        terms = weight_terms.astype(jnp.bfloat16).reshape(deep // part, part, channels)
+        input_grad, weight_total = conv_and_sum(pair_gradient, terms, weights, groups)
+        weight_total = weight_total.astype(jnp.float32)
     else:
         bordered_gradient = extended(pair_gradient, (("row", 0), ("col", 1)), DILATION_LIMIT)
         input_grad = conv_input_grad(bordered_gradient, weights, row_count, col_count)

time: 151 us -> 148 us (0.980); the launches traced: 148 us -> 147 us
  local copies, waits for them, and re-layouts: 9.77 us -> 8 us
where the time goes in v4:
time: 148 us; the launch traced here: 147 us
  Pallas kernels  115 us (78%)
  matrix products  15.8 us (11%)
  local copies, waits for them, and re-layouts  8 us (5%)
  other arithmetic  6.43 us (4%)
    pallas_call x1, Pallas kernels, triangle_product(): pl.pallas_call(functools.partial(product_kernel, groups, share, rows, col...  43.6 us
    pallas_call x1, Pallas kernels, triangle_back(): pl.pallas_call(functools.partial(back_kernel, groups, share, rows, cols),...  37.4 us
    pallas_call x1, Pallas kernels, conv_and_sum(): pl.pallas_call(functools.partial(last_kernel, groups, rows, cols), out_sh...  34.4 us
    unnamed x76, local copies, waits for them, and re-layouts  6.81 us
    dot_general x1, matrix products, on_device(): jnp.einsum('rkd,cd->rkc', grad_gate, out_gate_weight, preferred_element_t...  3.05 us

profile of v4, /device:TPU:0, one launch (start us, length us, event | category | flops | bytes accessed | tf_op | source)
XLA Modules:
  0.0 146.9 jit_solution(9963469798570923278)
XLA Ops:
  0.7 1.3 convert_reduce_fusion
  2.0 1.7 %fusion.28 = f32[8,256]{1,0:T(8,128)S(1)} fusion(bf16[8,256,128]{2,1,0:T(8,128)(2,1)} %param.15, f32[8,256]{1,0:T(8,128)S(1)} %broadcast_multiply_fusion.5), kind=kLoop, calls=%fused_computation.43 | loop fusion | flops 1046528 | bytes 540672 | tf_op jit(solution)/shard_map/reduce_sum | solution.py:32
  3.8 1.8 %fusion.9 = f32[8,256,128]{2,1,0:T(8,128)} fusion(bf16[128,128]{1,0:T(8,128)(2,1)S(1)} %copy-done.13, bf16[8,256,128]{2,1,0:T(8,128)(2,1)S(1)} %copy-done.4, f32[128]{0:T(128)S(1)} %copy-done.16, f32[128]{0:T(128)S(1)} %copy-done.14, f32[8,256]{1,0:T(8,128)S(1)} %add_rsqrt_fusion.1, f32[8,256]{1,0:T(8,128)S(1)} %broadcast_multiply_fusion.5), kind=kOutput, calls=%fused_computation.22 | convolution fusion | flops 69468160 | bytes 1623040 | tf_op jit(solution)/shard_map/rkc,cd->rkd/dot_general | solution.py:642
  5.6 0.1 copy.27
  5.7 1.6 %fusion.56 = f32[8,256,256]{1,2,0:T(8,128)S(1)} fusion(bf16[128,256,1]{0,1,2:T(8,128)(2,1)S(1)} %bitcast.221, bf16[8,256,128]{2,1,0:T(8,128)(2,1)S(1)} %copy-done.4, f32[128]{0:T(128)S(1)} %copy-done.16, f32[128]{0:T(128)S(1)} %copy-done.14, f32[8,256]{1,0:T(8,128)S(1)} %add_rsqrt_fusion.1, f32[8,256]{1,0:T(8,128)S(1)} %broadcast_multiply_fusion.5), kind=kOutput, calls=%fused_computation.139 | convolution fusion | flops 135790592 | bytes 2704384 | tf_op jit(solution)/shard_map/rkc,ce->erk/dot_general | solution.py:603
  7.4 0.3 fusion.20
  7.7 0.1 copy.28
  7.9 0.9 copy-done.5
  8.7 2.4 %fusion.1 = (bf16[256,8,256]{2,0,1:T(8,128)(2,1)S(1)}, f32[8,256,256]{1,2,0:T(8,128)}) fusion(f32[8,256,256]{1,2,0:T(8,128)S(1)} %fusion.56, f32[8,256]{1,0:T(8,128)S(1)} %fusion.20, bf16[128,256,1]{0,1,2:T(8,128)(2,1)S(1)} %bitcast.223, bf16[8,256,128]{2,1,0:T(8,128)(2,1)S(1)} %copy-done.4, f32[128]{0:T(128)S(1)} %copy-done.16, f32[128]{0:T(128)S(1)} %copy-done.14, ...), kind=kOutput, calls=%fused_computation.6 | convolution fusion | flops 138936320 | bytes 5858304 | tf_op jit(solution)/shard_map/rkc,ce->erk/dot_general | solution.py:606
  11.2 0.6 copy.29
  11.8 0.5 copy-done.1
  12.2 43.6 %triangle_product.1 = (bf16[32,32,256]{2,1,0:T(8,128)(2,1)S(1)}, bf16[4,2,256,256]{3,2,1,0:T(8,128)(2,1)S(1)}, bf16[2048,1152]{1,0:T(8,128)(2,1)S(1)}) custom-call(bf16[32,4,16,256]{3,2,1,0:T(8,128)(2,1)S(1)} %bitcast.210, bf16[8,256,128]{2,1,0:T(8,128)(2,1)S(1)} %copy-done.1, s32[1,128]{1,0:T(1,128)S(1)} %bitcast.216), custom_call_target="tpu_custom_call" | custom-call | tf_op jit(solution)/shard_map/triangle_product/pallas_call | solution.py:161
  55.8 2.1 %copy-done.3 = bf16[2048,1152]{1,0:T(8,128)(2,1)} copy-done((bf16[2048,1152]{1,0:T(8,128)(2,1)}, bf16[2048,1152]{1,0:T(8,128)(2,1)S(1)}, u32[]{:S(2)}) %copy-start.3) | copy-done | bytes 4718616
  58.1 0.1 convert_reduce_fusion.1
  58.2 0.3 multiply_reduce_fusion.1
  58.6 0.5 copy-done.8
  59.1 3.0 %fusion.19 = f32[8,256,128]{2,1,0:T(8,128)} fusion(f32[8,256,128]{2,1,0:T(8,128)} %fusion.9, bf16[8,256,128]{2,1,0:T(8,128)(2,1)S(1)} %copy-done.8, f32[128,8,256]{2,1,0:T(8,128)S(1)} %convert.2, f32[128]{0:T(128)S(1)} %copy-done.17, f32[128]{0:T(128)S(1)} %copy-done.15, f32[8,256]{1,0:T(8,128)S(1)} %add_rsqrt_fusion, ...), kind=kOutput, calls=%fused_computation.35 | convolution fusion | flops 137101312 | bytes 3752960 | tf_op jit(solution)/shard_map/rkd,cd->rkc/dot_general | solution.py:679
  62.1 1.9 %fusion.65 = (f32[8,256]{1,0:T(8,128)S(1)}, f32[8,256]{1,0:T(8,128)S(1)}, f32[128,8,256]{2,0,1:T(8,128)S(1)}) fusion(f32[8,256]{1,0:T(8,128)S(1)} %add_rsqrt_fusion, f32[8,256]{1,0:T(8,128)S(1)} %broadcast_multiply_fusion.4, f32[128,8,256]{2,1,0:T(8,128)S(1)} %convert.2, f32[128]{0:T(128)S(1)} %copy-done.15, bf16[128,128]{1,0:T(8,128)(2,1)S(1)} %copy-done, ...), kind=kOutput, calls=%fused_computation.166 | convolution fusion | flops 69464064 | bytes 3736064 | tf_op jit(solution)/shard_map/rkd,cd->crk/dot_general | solution.py:647
  64.0 0.5 multiply_convert_fusion
  64.5 0.3 copy.31
  64.8 37.4 %triangle_back.1 = bf16[32,4,16,256]{3,2,1,0:T(8,128)(2,1)S(1)} custom-call(bf16[32,32,256]{2,1,0:T(8,128)(2,1)S(1)} %bitcast.213, bf16[4,2,256,256]{3,2,1,0:T(8,128)(2,1)S(1)} %get-tuple-element.8.sides_ref), custom_call_target="tpu_custom_call" | custom-call | tf_op jit(solution)/shard_map/triangle_back/pallas_call | solution.py:192
  102.2 0.2 convert.3
  102.4 1.4 copy-done.7
  103.8 1.1 fusion.31
  104.9 2.3 %fusion.64 = (f32[8,256]{1,0:T(8,128)S(1)}, f32[8,256]{1,0:T(8,128)S(1)}, f32[8,256,128]{2,1,0:T(8,128)S(1)}) fusion(f32[8,256]{1,0:T(8,128)S(1)} %add_rsqrt_fusion.1, f32[8,256]{1,0:T(8,128)S(1)} %broadcast_multiply_fusion.5, bf16[8,256,128]{2,1,0:T(8,128)(2,1)S(1)} %copy-done.4, f32[128]{0:T(128)S(1)} %copy-done.14, f32[8,256,128]{2,1,0:T(8,128)S(1)} %copy-done.9, ...), kind=kOutput, calls=%fused_computation.165 | convolution fusion | flops 139718656 | bytes 10068480 | tf_op jit(solution)/shard_map/erk,ce->rkc/dot_general | solution.py:676
  107.2 1.3 fusion.30.grad_ref
  108.5 1.4 convolution_convert_fusion
  110.0 0.2 copy.37
  110.2 0.1 broadcast_select_fusion
  110.8 34.4 %conv_and_sum.1 = (bf16[8,256,128]{2,1,0:T(8,128)(2,1)S(1)}, bf16[24,48,128]{2,1,0:T(8,128)(2,1)S(1)}) custom-call(bf16[8,256,128]{2,1,0:T(8,128)(2,1)S(1)} %fusion.30.grad_ref, bf16[24,48,128]{2,1,0:T(8,128)(2,1)S(1)} %bitcast.215, bf16[4224,128]{1,0:T(8,128)(2,1)S(1)} %constant_dynamic-update-slice_fusion.weight_ref), custom_call_target="tpu_custom_call" | custom-call | tf_op jit(solution)/shard_map/conv_and_sum/pallas_call | solution.py:431
  145.2 0.9 convert_multiply_fusion.2
  146.1 0.8 copy.99
  (84 shorter events, 0.6 us)
Async XLA Ops:
  0.6 57.9 %copy-start = (bf16[128,128]{1,0:T(8,128)(2,1)S(1)}, bf16[128,128]{1,0:T(8,128)(2,1)}, u32[]{:S(2)}) copy-start(bf16[128,128]{1,0:T(8,128)(2,1)} %param.25) | copy-start | bytes 98308
  0.6 3.1 %copy-start.4 = (bf16[8,256,128]{2,1,0:T(8,128)(2,1)S(1)}, bf16[8,256,128]{2,1,0:T(8,128)(2,1)}, u32[]{:S(2)}) copy-start(bf16[8,256,128]{2,1,0:T(8,128)(2,1)} %param.15) | copy-start | bytes 1572868
  0.7 3.1 %copy-start.14 = (f32[128]{0:T(128)S(1)}, f32[128]{0:T(128)}, u32[]{:S(2)}) copy-start(f32[128]{0:T(128)} %param.19) | copy-start | bytes 1540
  0.7 3.1 %copy-start.13 = (bf16[128,128]{1,0:T(8,128)(2,1)S(1)}, bf16[128,128]{1,0:T(8,128)(2,1)}, u32[]{:S(2)}) copy-start(bf16[128,128]{1,0:T(8,128)(2,1)} %param.26) | copy-start | bytes 98308
  0.7 3.1 %copy-start.16 = (f32[128]{0:T(128)S(1)}, f32[128]{0:T(128)}, u32[]{:S(2)}) copy-start(f32[128]{0:T(128)} %param.20) | copy-start | bytes 1540
  3.7 1.8 %copy-start.11 = (bf16[128,256]{1,0:T(8,128)(2,1)S(1)}, bf16[128,256]{1,0:T(8,128)(2,1)}, u32[]{:S(2)}) copy-start(bf16[128,256]{1,0:T(8,128)(2,1)} %param.21) | copy-start | bytes 196612
  5.7 1.7 %copy-start.18 = (s32[2,2]{1,0:T(2,128)S(1)}, s32[2,2]{1,0:T(2,128)}, u32[]{:S(2)}) copy-start(s32[2,2]{1,0:T(2,128)} %param.17) | copy-start | bytes 52
  5.7 2.0 %copy-start.12 = (bf16[128,256]{1,0:T(8,128)(2,1)S(1)}, bf16[128,256]{1,0:T(8,128)(2,1)}, u32[]{:S(2)}) copy-start(bf16[128,256]{1,0:T(8,128)(2,1)} %param.22) | copy-start | bytes 196612
  7.4 1.4 copy-start.5
  11.2 1.0 copy-start.1
  11.2 1.0 copy-start.2
  55.8 2.1 %copy-start.3 = (bf16[2048,1152]{1,0:T(8,128)(2,1)}, bf16[2048,1152]{1,0:T(8,128)(2,1)S(1)}, u32[]{:S(2)}) copy-start(bf16[2048,1152]{1,0:T(8,128)(2,1)S(1)} %get-tuple-element.9) | copy-start | bytes 14155780
  58.0 1.0 copy-start.8
  58.0 1.0 copy-start.15
  58.0 1.0 copy-start.17
  102.2 1.6 %copy-start.7 = (f32[8,256,256]{1,2,0:T(8,128)S(1)}, f32[8,256,256]{1,2,0:T(8,128)}, u32[]{:S(2)}) copy-start(f32[8,256,256]{1,2,0:T(8,128)} %get-tuple-element.25) | copy-start | bytes 6291460
  102.2 2.7 %copy-start.6 = (f32[8,256,256]{1,2,0:T(8,128)S(1)}, f32[8,256,256]{1,2,0:T(8,128)}, u32[]{:S(2)}) copy-start(f32[8,256,256]{1,2,0:T(8,128)} %copy-done.5) | copy-start | bytes 6291460
  102.2 2.7 %copy-start.9 = (f32[8,256,128]{2,1,0:T(8,128)S(1)}, f32[8,256,128]{2,1,0:T(8,128)}, u32[]{:S(2)}) copy-start(f32[8,256,128]{2,1,0:T(8,128)} %fusion.19) | copy-start | bytes 3145732
  103.8 4.7 %slice-start = ((s8[4718592]{0:T(1024)(128)(4,1)}), s8[4194304]{0:T(1024)(128)(4,1)S(1)}, s32[]{:S(2)}) async-start(s8[4718592]{0:T(1024)(128)(4,1)} %bitcast.217), calls=%async_computation | async-start | bytes 8388608
  104.9 3.6 %slice-start.1 = ((s8[4718592]{0:T(1024)(128)(4,1)}), s8[524288]{0:T(1024)(128)(4,1)S(1)}, s32[]{:S(2)}) async-start(s8[4718592]{0:T(1024)(128)(4,1)} %bitcast.217), calls=%async_computation.1 | async-start | bytes 1048576
  108.5 1.5 %copy-start.10 = (bf16[9,128,128]{2,1,0:T(8,128)(2,1)S(1)}, bf16[9,128,128]{2,1,0:T(8,128)(2,1)}, u32[]{:S(2)}) copy-start(bf16[9,128,128]{2,1,0:T(8,128)(2,1)} %param.27) | copy-start | bytes 884740
